TPU v7x, 512 devices: a whole 4x4x16 slice. The times are simulated.
512 devices in a mesh: seq: 64 (over x, z), tp: 8 (over y, core).
Axes of the slice: x: 4, y: 4, z: 16, core: 2. Of those that a mesh axis runs over, the one named last changes fastest.
Arguments:
- streams: bfloat16 [3, 8192, 16384], P(None, 'tp', 'seq'), may hold values from -6 to 6
- short_taps: float32 [3, 8192, 7], P(None, 'tp'), may hold values from -2 to 2
- long_taps: float32 [512, 128], P('tp'), may hold values from -0.5 to 0.5
- doc_marks: int32 [16384], P('seq'), may hold values 0 or 1
- upstream: bfloat16 [8192, 16384], P('tp', 'seq'), may hold values from -6 to 6
Outputs:
- mixed_out: bfloat16 [8192, 16384], P('tp', 'seq')
- grad_streams: bfloat16 [3, 8192, 16384], P(None, 'tp', 'seq')
- grad_long: float32 [512, 128], P('tp')
- grad_short: float32 [3, 8192, 7], P(None, 'tp')
All inputs are finite; a program needn't handle non-finite values. No bound on the sum of `doc_marks` on one device may be relied on, other than what follows from the above.
Results may differ from a plain program's by a relative error of at most 0.015.
Values may be sent and summed in bfloat16 or wider, within the bound.
No kernel may reach another device: no remote copies, remote signals or barrier semaphores. Data moves between devices by JAX's collectives and lax.ppermute only.
A program may use at most 64 MiB of HBM per device.

v0:
```python
import math

import jax
import jax.numpy as jnp
from jax import lax
from jax.sharding import PartitionSpec as P


def from_behind(block, axis, distance):
    devices = range(lax.axis_size(axis))
    route = [(i - distance, i) for i in devices if i - distance in devices]
    return lax.ppermute(block, axis, route)


def band_table(filt, rows, width, forward):
    count = filt.shape[0]
    taps = filt.shape[1]
    if forward:
        base = jnp.concatenate(
            [
                jnp.zeros((count, 1), filt.dtype),
                filt[:, ::-1],
                jnp.zeros((count, width - taps), filt.dtype),
            ],
            axis=1,
        )
    else:
        base = jnp.concatenate([filt, jnp.zeros((count, width + 1 - taps), filt.dtype)], axis=1)
    tiled = jnp.tile(base, (1, rows))[:, : rows * width]
    return tiled.reshape(count, rows, width)


def diagonal_sums(product, taps):
    count, rows, width = product.shape
    flat = jnp.pad(product.reshape(count, rows * width), ((0, 0), (0, rows)))
    folded = jnp.sum(flat.reshape(count, rows, width + 1), axis=1)
    return folded[:, 1 : taps + 1][:, ::-1]


def featurize(raw_win, weights, starts_win, first_pos, edge):
    count = raw_win.shape[2] - edge
    spots = first_pos + edge + jnp.arange(count, dtype=jnp.int32)
    limits = starts_win[edge:]
    total = jnp.zeros(raw_win.shape[:2] + (count,), jnp.float32)
    for lag in range(edge + 1):
        keep = (spots - lag >= limits).astype(jnp.float32)
        piece = raw_win[:, :, edge - lag : edge - lag + count].astype(jnp.float32)
        total = total + weights[:, :, lag : lag + 1] * piece * keep
    return total.astype(jnp.bfloat16)


def local(streams, short_taps, long_taps, doc_marks, upstream):
    tok = streams.shape[2]
    chan = streams.shape[1]
    groups = long_taps.shape[0]
    taps = long_taps.shape[1]
    short = short_taps.shape[2]
    edge = short - 1
    extra = taps + edge
    members = chan // groups
    width = tok + taps
    anchor = lax.axis_index("seq") * tok
    places = anchor + jnp.arange(tok, dtype=jnp.int32)
    marks_bf = doc_marks.astype(jnp.bfloat16)
    raw_tail, mark_tail = from_behind(
        (streams[:, :, tok - edge :], marks_bf[tok - extra :]), "seq", 1
    )
    q_tail = raw_tail[0:1]
    kv_tail = raw_tail[1:]
    window_pos = anchor - extra + jnp.arange(extra + tok, dtype=jnp.int32)
    window_marks = jnp.concatenate([mark_tail, marks_bf])
    win_starts = lax.cummax(jnp.where(window_marks == 1, window_pos, -1), axis=0)
    local_starts = win_starts[extra:]
    q_raw = jnp.concatenate([q_tail, streams[0:1]], axis=2)
    feat_q = featurize(q_raw, short_taps[0:1], win_starts[taps:], anchor - edge, edge)[0]
    kv_raw = jnp.concatenate([kv_tail, streams[1:]], axis=2)
    feat_kv = featurize(kv_raw, short_taps[1:], win_starts[taps:], anchor - edge, edge)
    feat_k = feat_kv[0]
    feat_v = feat_kv[1]
    mixed = (feat_k.astype(jnp.float32) * feat_v.astype(jnp.float32)).astype(jnp.bfloat16)
    mixed_tail = from_behind(mixed[:, tok - taps :], "seq", 1)
    mixed_win = jnp.concatenate([mixed_tail, mixed], axis=1)
    raw_all = jnp.concatenate([q_raw, kv_raw], axis=0)
    gate_grad = (upstream.astype(jnp.float32) * feat_q.astype(jnp.float32)).astype(jnp.bfloat16)
    gate_head, mark_head = from_behind((gate_grad[:, :taps], marks_bf[:taps]), "seq", -1)
    gate_win = jnp.concatenate([gate_grad, gate_head], axis=1)
    back_pos = anchor + jnp.arange(width, dtype=jnp.int32)
    back_marks = jnp.concatenate([marks_bf, mark_head])
    back_starts = lax.cummax(jnp.where(back_marks == 1, back_pos, -1), axis=0)
    block_cols = 2 * taps
    nblocks = tok // taps
    rows = jnp.arange(taps, dtype=jnp.int32)[:, None]
    cols = jnp.arange(block_cols, dtype=jnp.int32)[None, :]
    lag_grid = cols - rows
    band = (lag_grid >= 1) & (lag_grid <= taps)
    fwd_masks = []
    back_masks = []
    for blk in range(nblocks):
        low = blk * taps
        own = local_starts[low : low + taps]
        fwd_masks.append(band & (anchor - taps + low + cols >= own[:, None]))
        later = back_starts[low : low + block_cols]
        back_masks.append(places[low : low + taps][:, None] >= later[None, :])
    batch = math.gcd(16, groups)
    rounds = groups // batch
    filt_bf = long_taps.astype(jnp.bfloat16)
    mixed_parts = mixed_win.reshape(rounds, batch, members, width)
    gate_parts = gate_grad.reshape(rounds, batch, members, tok)
    gwin_parts = gate_win.reshape(rounds, batch, members, width)
    filt_parts = filt_bf.reshape(rounds, batch, taps)
    zero_bf = jnp.zeros((), jnp.bfloat16)

    def group_step(operands):
        mixed_part, gate_part, gwin_part, filt_part = operands
        forward_base = band_table(filt_part, taps, block_cols, True)
        backward_base = band_table(filt_part, taps, block_cols, False)
        conv_list = []
        back_list = []
        filt_acc = jnp.zeros((filt_part.shape[0], taps), jnp.float32)
        for blk in range(nblocks):
            low = blk * taps
            mixed_blk = mixed_part[:, :, low : low + block_cols]
            forward_table = jnp.where(fwd_masks[blk][None], forward_base, zero_bf)
            conv_list.append(
                jnp.einsum(
                    "gcj,gtj->gct", mixed_blk, forward_table, preferred_element_type=jnp.float32
                )
            )
            backward_table = jnp.where(back_masks[blk][None], backward_base, zero_bf)
            back_list.append(
                jnp.einsum(
                    "gct,git->gci",
                    gwin_part[:, :, low : low + block_cols],
                    backward_table,
                    preferred_element_type=jnp.float32,
                )
            )
            product = jnp.einsum(
                "gct,gcj->gtj",
                gate_part[:, :, low : low + taps],
                mixed_blk,
                preferred_element_type=jnp.float32,
            )
            product = jnp.where(fwd_masks[blk][None], product, 0.0)
            filt_acc = filt_acc + diagonal_sums(product, taps)
        return (jnp.concatenate(conv_list, axis=2), jnp.concatenate(back_list, axis=2), filt_acc)

    conv, back, filt_grad = lax.map(group_step, (mixed_parts, gate_parts, gwin_parts, filt_parts))
    conv = conv.reshape(chan, tok)
    back = back.reshape(chan, tok)
    filt_grad = filt_grad.reshape(groups, taps)
    mixed_out = (feat_q.astype(jnp.float32) * conv).astype(jnp.bfloat16)
    grad_q = (upstream.astype(jnp.float32) * conv).astype(jnp.bfloat16)
    grad_k = (back * feat_v.astype(jnp.float32)).astype(jnp.bfloat16)
    grad_v = (back * feat_k.astype(jnp.float32)).astype(jnp.bfloat16)
    feat_grad = jnp.stack([grad_q, grad_k, grad_v])
    feat_head = from_behind(feat_grad[:, :, :edge], "seq", -1)
    grad_win = jnp.concatenate([feat_grad, feat_head], axis=2)
    total = jnp.zeros((3, chan, tok), jnp.float32)
    columns = []
    for lag in range(short):
        keep = (places >= back_starts[lag : lag + tok]).astype(jnp.float32)
        total = (
            total
            + short_taps[:, :, lag : lag + 1]
            * grad_win[:, :, lag : lag + tok].astype(jnp.float32)
            * keep
        )
        valid = (places - lag >= local_starts).astype(jnp.float32)
        piece = raw_all[:, :, edge - lag : edge - lag + tok].astype(jnp.float32)
        columns.append(jnp.sum(feat_grad.astype(jnp.float32) * piece * valid, axis=2))
    grad_streams = total.astype(jnp.bfloat16)
    short_grad = jnp.stack(columns, axis=2)
    filt_total, short_total = lax.psum((filt_grad, short_grad), "seq")
    square_sum = jnp.sum(filt_total * filt_total) + jnp.sum(short_total * short_total)
    square_all = lax.psum(square_sum, "tp")
    entries = groups * lax.axis_size("tp") * taps + 3 * chan * lax.axis_size("tp") * short
    scale = jnp.minimum(1.0, 1.0 / jnp.sqrt(square_all / entries + 1e-06))
    return (mixed_out, grad_streams, filt_total * scale, short_total * scale)


def solution(mesh):
    in_specs = (P(None, "tp", "seq"), P(None, "tp", None), P("tp", None), P("seq"), P("tp", "seq"))
    out_specs = (P("tp", "seq"), P(None, "tp", "seq"), P("tp", None), P(None, "tp", None))
    return jax.shard_map(local, mesh=mesh, in_specs=in_specs, out_specs=out_specs, check_vma=False)
```

profile of v0, /device:TPU:1, one launch (start us, length us, event | category | flops | bytes accessed | tf_op | source)
XLA Modules:
  0.0 503.9 jit_solution(17862456565224048816)
XLA Ops:
  8.6 4.9 collective-permute-start
  13.5 1.4 slice.323
  15.2 3.2 collective-permute-start.1
  18.4 1.3 collective-permute-start.4
  27.9 4.8 fusion.51
  32.6 1.0 slice.436
  33.6 1.3 collective-permute-start.3
  35.2 5.1 %add_convert_fusion = bf16[2,1024,256]{2,1,0:T(8,128)(2,1)S(1)} fusion(bf16[2,1024,256]{2,1,0:T(8,128)(2,1)S(1)} %slice.337, bf16[2,1024,6]{2,1,0:T(8,128)(2,1)S(1)} %copy.24, f32[256]{0:T(256)S(1)} %get-tuple-element.316, f32[2,1024]{1,0:T(2,128)S(1)} %get-tuple-element.324, f32[256]{0:T(256)S(1)} %get-tuple-element.317, ...), kind=kLoop, calls=%fused_computation.77 | loop fusion | flops 24117248 | bytes 2186240 | tf_op jit(solution)/shard_map/convert_element_type | solution.py:49
  40.4 1.0 copy-done.2
  41.6 4.8 collective-permute-start.2
  46.4 2.5 maximum_maximum_fusion.1
  48.9 2.0 pad_maximum_fusion.4
  50.9 1.0 pad_maximum_fusion.3
  51.9 109.8 %while.17 = (s32[]{:T(128)}, f32[4,16,16,256]{3,2,1,0:T(8,128)}, f32[4,16,16,256]{3,2,1,0:T(8,128)}, f32[4,16,128]{2,1,0:T(8,128)}, bf16[4,16,16,384]{3,2,1,0:T(...) while((s32[]{:T(128)}, f32[4,16,16,256]{3,2,1,0:T(8,128)}, ...), condition=%wide.region_7.8_spmd.clone, body=%wide.region_4.7_spmd.clone.sunk | while | flops 105470016 | bytes 62892232 | solution.py:148
  52.4 1.8 tile.33
  55.6 1.0 dynamic-slice_bitcast_fusion.9
  57.5 1.8 tile.35
  60.7 1.0 dynamic-slice_bitcast_fusion.10
  64.7 1.2 copy.69
  65.9 1.4 pad.230
  67.4 3.7 reshape.225
  71.9 1.2 copy.70
  73.2 1.4 pad.231
  74.6 3.7 reshape.226
  79.8 1.8 tile.33
  83.0 1.0 dynamic-slice_bitcast_fusion.9
  84.9 1.8 tile.35
  92.1 1.2 copy.69
  93.4 1.4 pad.230
  94.8 3.7 reshape.225
  99.4 1.2 copy.70
  100.6 1.4 pad.231
  102.1 3.7 reshape.226
  107.3 1.8 tile.33
  112.4 1.8 tile.35
  115.6 1.0 dynamic-slice_bitcast_fusion.10
  119.6 1.2 copy.69
  120.8 1.4 pad.230
  122.3 3.7 reshape.225
  126.8 1.2 copy.70
  128.1 1.4 pad.231
  129.5 3.7 reshape.226
  134.7 1.8 tile.33
  137.9 1.0 dynamic-slice_bitcast_fusion.9
  139.8 1.8 tile.35
  147.1 1.2 copy.69
  148.3 1.4 pad.230
  149.7 3.7 reshape.225
  154.3 1.2 copy.70
  155.5 1.4 pad.231
  157.0 3.7 reshape.226
  161.8 1.8 fusion.49
  163.9 1.0 fusion.50
  165.6 5.6 %fusion.46 = (f32[3,1024]{1,0:T(4,128)S(1)}, f32[3,1024]{1,0:T(4,128)S(1)}, f32[3,1024]{1,0:T(4,128)S(1)}, f32[3,1024]{1,0:T(4,128)S(1)}, f32[3,1024]{1,0:T(4,128)S(1)}, /*index=5*/f32[3,1024]{1,0:T(4,128)S(1)}) fusion(bf16[3,1024,262]{2,1,0:T(8,128)(2,1)S(1)} %copy-done, f32[256]{0:T(256)S(1)} %copy-done.23, ...), kind=kLoop, calls=%fused_computation.69 | loop fusion | flops 21215232 | bytes 11089920 | tf_op jit(solution)/shard_map/reduce_sum | solution.py:171
  171.2 1.6 fusion.34
  173.8 230.3 %psum.21 = f32[64,128]{1,0:T(8,128)S(1)} all-reduce(f32[64,128]{1,0:T(8,128)S(1)} %bitcast.172), channel_id=1, replica_groups=mesh['seq'=64,'tp'=8] {'seq'}, use_global_device_ids=true, to_apply=%region_8.9 | all-reduce | flops 8192 | bytes 65536 | tf_op jit(solution)/shard_map/psum | solution.py:174
  404.5 1.3 collective-permute-start.5
  406.4 3.2 collective-permute-done.5
  409.6 1.2 copy.26
  410.9 1.6 pad_maximum_fusion
  412.4 19.8 %all-reduce.6.cloned.1.call-done = f32[3,1024,7]{1,0,2:T(4,128)} async-done(((f32[3,1024,7]{1,0,2:T(4,128)}), f32[3,1024,7]{1,0,2:T(4,128)}) %all-reduce.6.cloned.1.call-update) | async-done | bytes 86032 | tf_op jit(solution)/shard_map/psum | solution.py:174
  432.2 1.6 multiply_reduce_fusion
  435.1 8.8 %fusion.32 = bf16[3,1024,256]{2,1,0:T(8,128)(2,1)} fusion(bf16[3,1024,262]{2,1,0:T(8,128)(2,1)S(1)} %pad_maximum_fusion, f32[256]{0:T(256)} %get-tuple-element.306, f32[3,1024]{1,0:T(4,128)} %get-tuple-element.332, f32[256]{0:T(256)} %get-tuple-element.307, f32[3,1024]{1,0:T(4,128)} %get-tuple-element.333, f32[256]{0:T(256)} %get-tuple-element.308, ...), kind=kLoop, calls=%fused_computation.55 | loop fusion | flops 23592960 | bytes 12676096 | tf_op jit(solution)/shard_map/convert_element_type | solution.py:172
  443.9 51.1 %psum.23 = f32[]{:T(128)} all-reduce(f32[]{:T(128)S(6)} %add.180), channel_id=1, replica_groups=mesh['seq'=64,'tp'=8] {'tp'}, use_global_device_ids=true, to_apply=%region_19.20 | all-reduce | flops 1 | bytes 8 | tf_op jit(solution)/shard_map/psum | solution.py:176
  (324 shorter events, 52.5 us)
Async XLA Ops:
  7.2 12.5 %copy-start.3 = (bf16[3,1024,256]{2,1,0:T(8,128)(2,1)S(1)}, bf16[3,1024,256]{2,1,0:T(8,128)(2,1)}, u32[]{:S(2)}) copy-start(bf16[3,1024,256]{2,1,0:T(8,128)(2,1)} %param.7) | copy-start | bytes 4718596
  7.2 12.6 %copy-start.8 = (f32[3,1024,7]{1,2,0:T(8,128)S(1)}, f32[3,1024,7]{1,2,0:T(8,128)}, u32[]{:S(2)}) copy-start(f32[3,1024,7]{1,2,0:T(8,128)} %param.8) | copy-start | bytes 258052
  7.2 425.0 %all-reduce.6.cloned.1.call-start = ((), (), s32[]{:S(2)}) async-start(), calls=%async_computation | async-start | bytes 229376 | tf_op jit(solution)/shard_map/psum | solution.py:174
  8.0 15.6 %copy-start.34 = (bf16[256]{0:T(256)(128)(2,1)}, bf16[256]{0:T(256)(128)(2,1)S(1)}, u32[]{:S(2)}) copy-start(bf16[256]{0:T(256)(128)(2,1)S(1)} %convert_element_type.218) | copy-start | bytes 1540
  8.6 16.9 %collective-permute-start = (bf16[134]{0:T(256)(128)(2,1)}, bf16[134]{0:T(256)(128)(2,1)}, u32[]{:S(2)}, u32[]{:S(2)}) collective-permute-start(bf16[134]{0:T(256)(128)(2,1)} %slice.318), channel_id=1, source_target_pairs={{0,8},{8,16},{16,24},{24,32},{32,40},{40,48},{48,56},{56,64},{64,7... | collective-permute-start | bytes 812 | tf_op jit(solution)/shard_map/ppermute | solution.py:12
  15.2 7.8 %copy-start.14 = (f32[64,128]{1,0:T(8,128)S(1)}, f32[64,128]{1,0:T(8,128)}, u32[]{:S(2)}) copy-start(f32[64,128]{1,0:T(8,128)} %param.9) | copy-start | bytes 98308
  15.2 12.4 %collective-permute-start.1 = (bf16[3,1024,6]{1,2,0:T(8,128)(2,1)S(1)}, bf16[3,1024,6]{1,2,0:T(8,128)(2,1)S(1)}, u32[]{:S(2)}, u32[]{:S(2)}) collective-permute-start(bf16[3,1024,6]{1,2,0:T(8,128)(2,1)S(1)} %copy.42), channel_id=1, source_target_pairs={{0,8},{8,16},{16,24},{24,32},{32,40},{40,48},{48,56},{56,64},{64,7... | collective-permute-start | bytes 110600 | tf_op jit(solution)/shard_map/ppermute | solution.py:12
  18.4 5.3 %collective-permute-start.4 = (bf16[128]{0:T(256)(128)(2,1)S(1)}, bf16[128]{0:T(256)(128)(2,1)S(1)}, u32[]{:S(2)}, u32[]{:S(2)}) collective-permute-start(bf16[128]{0:T(256)(128)(2,1)S(1)} %bitcast.180), channel_id=1, source_target_pairs={{8,0},{16,8},{24,16},{32,24},{40,32},{48,40},{56,48},{64,56},{72,6... | collective-permute-start | bytes 776 | tf_op jit(solution)/shard_map/ppermute | solution.py:12
  27.0 13.4 %copy-start.20 = (f32[256]{0:T(256)}, f32[256]{0:T(256)S(1)}, u32[]{:S(2)}) copy-start(f32[256]{0:T(256)S(1)} %get-tuple-element.315) | copy-start | bytes 3076
  27.0 13.4 %copy-start.22 = (f32[256]{0:T(256)}, f32[256]{0:T(256)S(1)}, u32[]{:S(2)}) copy-start(f32[256]{0:T(256)S(1)} %get-tuple-element.316) | copy-start | bytes 3076
  27.0 13.4 %copy-start.24 = (f32[256]{0:T(256)}, f32[256]{0:T(256)S(1)}, u32[]{:S(2)}) copy-start(f32[256]{0:T(256)S(1)} %get-tuple-element.317) | copy-start | bytes 3076
  27.0 13.4 %copy-start.26 = (f32[256]{0:T(256)}, f32[256]{0:T(256)S(1)}, u32[]{:S(2)}) copy-start(f32[256]{0:T(256)S(1)} %get-tuple-element.318) | copy-start | bytes 3076
  27.0 13.4 %copy-start.28 = (f32[256]{0:T(256)}, f32[256]{0:T(256)S(1)}, u32[]{:S(2)}) copy-start(f32[256]{0:T(256)S(1)} %get-tuple-element.319) | copy-start | bytes 3076
  27.0 13.4 %copy-start.30 = (f32[256]{0:T(256)}, f32[256]{0:T(256)S(1)}, u32[]{:S(2)}) copy-start(f32[256]{0:T(256)S(1)} %get-tuple-element.320) | copy-start | bytes 3076
  27.0 13.4 %copy-start.32 = (f32[256]{0:T(256)}, f32[256]{0:T(256)S(1)}, u32[]{:S(2)}) copy-start(f32[256]{0:T(256)S(1)} %get-tuple-element.321) | copy-start | bytes 3076
  33.6 15.3 %collective-permute-start.3 = (bf16[1024,128]{1,0:T(8,128)(2,1)S(1)}, bf16[1024,128]{1,0:T(8,128)(2,1)S(1)}, u32[]{:S(2)}, u32[]{:S(2)}) collective-permute-start(bf16[1024,128]{1,0:T(8,128)(2,1)S(1)} %slice.436), channel_id=1, source_target_pairs={{8,0},{16,8},{24,16},{32,24},{40,32},{48,40},{56,48},{64,56},{72,6... | collective-permute-start | bytes 786440 | tf_op jit(solution)/shard_map/ppermute | solution.py:12
  40.4 1.0 copy-start.2
  41.6 9.3 %collective-permute-start.2 = (bf16[1024,128]{1,0:T(8,128)(2,1)S(1)}, bf16[1024,128]{1,0:T(8,128)(2,1)S(1)}, u32[]{:S(2)}, u32[]{:S(2)}) collective-permute-start(bf16[1024,128]{1,0:T(8,128)(2,1)S(1)} %slice.435), channel_id=1, source_target_pairs={{0,8},{8,16},{16,24},{24,32},{32,40},{40,48},{48,56},{56,64},{64,7... | collective-permute-start | bytes 786440 | tf_op jit(solution)/shard_map/ppermute | solution.py:12
  51.9 3.3 copy-start.18
  51.9 7.7 %copy-start.12 = (s32[256]{0:T(256)}, s32[256]{0:T(256)S(1)}, u32[]{:S(2)}) copy-start(s32[256]{0:T(256)S(1)} %get-tuple-element.499) | copy-start | bytes 3076 | tf_op jit(solution)/shard_map/while
  51.9 8.4 %copy-start.10 = (s32[256]{0:T(256)}, s32[256]{0:T(256)S(1)}, u32[]{:S(2)}) copy-start(s32[256]{0:T(256)S(1)} %get-tuple-element.501) | copy-start | bytes 3076 | tf_op jit(solution)/shard_map/while
  51.9 8.4 %copy-start.16 = (s32[128]{0:T(128)}, s32[128]{0:T(128)S(1)}, u32[]{:S(2)}) copy-start(s32[128]{0:T(128)S(1)} %get-tuple-element.502) | copy-start | bytes 1540 | tf_op jit(solution)/shard_map/while
  78.3 1.0 copy-start.11
  78.3 1.0 copy-start.13
  78.3 1.0 copy-start.17
  78.4 1.0 copy-start.19
  79.4 3.3 copy-start.18
  79.4 7.7 %copy-start.12 = (s32[256]{0:T(256)}, s32[256]{0:T(256)S(1)}, u32[]{:S(2)}) copy-start(s32[256]{0:T(256)S(1)} %get-tuple-element.499) | copy-start | bytes 3076 | tf_op jit(solution)/shard_map/while
  79.4 8.4 %copy-start.10 = (s32[256]{0:T(256)}, s32[256]{0:T(256)S(1)}, u32[]{:S(2)}) copy-start(s32[256]{0:T(256)S(1)} %get-tuple-element.501) | copy-start | bytes 3076 | tf_op jit(solution)/shard_map/while
  79.4 8.4 %copy-start.16 = (s32[128]{0:T(128)}, s32[128]{0:T(128)S(1)}, u32[]{:S(2)}) copy-start(s32[128]{0:T(128)S(1)} %get-tuple-element.502) | copy-start | bytes 1540 | tf_op jit(solution)/shard_map/while
  105.8 1.0 copy-start.11
  105.8 1.0 copy-start.13
  105.8 1.0 copy-start.17
  105.8 1.0 copy-start.19
  106.8 3.3 copy-start.18
  106.9 7.7 %copy-start.12 = (s32[256]{0:T(256)}, s32[256]{0:T(256)S(1)}, u32[]{:S(2)}) copy-start(s32[256]{0:T(256)S(1)} %get-tuple-element.499) | copy-start | bytes 3076 | tf_op jit(solution)/shard_map/while
  106.9 8.4 %copy-start.10 = (s32[256]{0:T(256)}, s32[256]{0:T(256)S(1)}, u32[]{:S(2)}) copy-start(s32[256]{0:T(256)S(1)} %get-tuple-element.501) | copy-start | bytes 3076 | tf_op jit(solution)/shard_map/while
  106.9 8.4 %copy-start.16 = (s32[128]{0:T(128)}, s32[128]{0:T(128)S(1)}, u32[]{:S(2)}) copy-start(s32[128]{0:T(128)S(1)} %get-tuple-element.502) | copy-start | bytes 1540 | tf_op jit(solution)/shard_map/while
  133.2 1.0 copy-start.11
  133.2 1.0 copy-start.13
  133.2 1.0 copy-start.17
  133.3 1.0 copy-start.19
  134.3 3.3 copy-start.18
  134.3 7.7 %copy-start.12 = (s32[256]{0:T(256)}, s32[256]{0:T(256)S(1)}, u32[]{:S(2)}) copy-start(s32[256]{0:T(256)S(1)} %get-tuple-element.499) | copy-start | bytes 3076 | tf_op jit(solution)/shard_map/while
  134.3 8.4 %copy-start.10 = (s32[256]{0:T(256)}, s32[256]{0:T(256)S(1)}, u32[]{:S(2)}) copy-start(s32[256]{0:T(256)S(1)} %get-tuple-element.501) | copy-start | bytes 3076 | tf_op jit(solution)/shard_map/while
  134.3 8.4 %copy-start.16 = (s32[128]{0:T(128)}, s32[128]{0:T(128)S(1)}, u32[]{:S(2)}) copy-start(s32[128]{0:T(128)S(1)} %get-tuple-element.502) | copy-start | bytes 1540 | tf_op jit(solution)/shard_map/while
  160.7 1.0 copy-start.11
  160.7 1.0 copy-start.13
  160.7 1.0 copy-start.17
  160.7 1.0 copy-start.19
  161.7 2.0 copy-start.4
  161.8 2.0 copy-start.5
  161.8 2.2 copy-start.6
  163.6 1.9 copy-start
  163.6 1.9 copy-start.23
  163.7 1.9 copy-start.25
  163.7 1.9 copy-start.27
  163.7 1.9 copy-start.29
  163.7 1.9 copy-start.31
  163.7 1.9 copy-start.33
  165.0 7.8 %copy-start.1 = (bf16[1024,256]{1,0:T(8,128)(2,1)}, bf16[1024,256]{1,0:T(8,128)(2,1)S(1)}, u32[]{:S(2)}) copy-start(bf16[1024,256]{1,0:T(8,128)(2,1)S(1)} %get-tuple-element.282) | copy-start | bytes 1572868
  165.6 5.6 %copy-start.21 = (f32[256]{0:T(256)S(1)}, f32[256]{0:T(256)}, u32[]{:S(2)}) copy-start(f32[256]{0:T(256)} %copy-done.20) | copy-start | bytes 3076
  404.5 5.1 %collective-permute-start.5 = (bf16[3,1024,6]{1,2,0:T(8,128)(2,1)S(1)}, bf16[3,1024,6]{1,2,0:T(8,128)(2,1)S(1)}, u32[]{:S(2)}, u32[]{:S(2)}) collective-permute-start(bf16[3,1024,6]{1,2,0:T(8,128)(2,1)S(1)} %copy.25), channel_id=1, source_target_pairs={{8,0},{16,8},{24,16},{32,24},{40,32},{48,40},{56,48},{64,56},{72,6... | collective-permute-start | bytes 110600 | tf_op jit(solution)/shard_map/ppermute | solution.py:12
  435.1 61.2 %copy-start.7 = (f32[3,1024,7]{1,0,2:T(4,128)S(1)}, f32[3,1024,7]{1,0,2:T(4,128)}, u32[]{:S(2)}) copy-start(f32[3,1024,7]{1,0,2:T(4,128)} %all-reduce.6.cloned.1.call-done) | copy-start | bytes 258052
  (2 other events, 1.6 us)
Sparse Core Ops, SparseCore 0:
  173.9 258.3 all-reduce.5
where the time goes:
time: 506 us; the launch traced here: 504 us
  blocking collectives  281 us (56%)
  local copies, waits for them, and re-layouts  96.3 us (19%)
  other arithmetic  58.7 us (12%)
  waiting for transfers between devices  23.1 us (5%)
  starting transfers between devices  16.8 us (3%)
  between operations  16.6 us (3%)
  matrix products  9.96 us (2%)
    psum x1, blocking collectives, local(): filt_total, short_total = lax.psum((filt_grad, short_grad), 'seq')  230 us
    psum x1, blocking collectives, local(): square_all = lax.psum(square_sum, 'tp')  51.1 us
    reshape x8, local copies, waits for them, and re-layouts, diagonal_sums(): folded = jnp.sum(flat.reshape(count, rows, width + 1), axis=1)  29.6 us
    psum x1, waiting for transfers between devices, local(): filt_total, short_total = lax.psum((filt_grad, short_grad), 'seq')  19.8 us
    ppermute x6, starting transfers between devices, from_behind(): return lax.ppermute(block, axis, route)  16.7 us
    another operation x16, local copies, waits for them, and re-layouts, band_table(): tiled = jnp.tile(base, (1, rows))[:, :rows * width]  16 us
    while x80, local copies, waits for them, and re-layouts  11.7 us
    pad x8, local copies, waits for them, and re-layouts, diagonal_sums(): flat = jnp.pad(product.reshape(count, rows * width), ((0, 0), (0, rows)))  11.6 us
  transfers between devices with their start and end apart: 7, of which 2 were waited for; matrix products, arithmetic and copies ran while one was open for 5% of the time, Pallas kernels for 0%

commit v1 on v0

v1 whole, which is shorter than its diff:
```python
import functools

import jax
import jax.numpy as jnp
from jax import lax
from jax.experimental import pallas as pl
from jax.experimental.pallas import tpu as pltpu
from jax.sharding import Mesh
from jax.sharding import PartitionSpec as P

BF = jnp.bfloat16
F32 = jnp.float32
SEQ = ("x", "zh", "zl")
TP = ("y", "c")
CUBE = ("x", "zl")
TILE = 128
EDGE_ROWS = 8
BLOCK = 256
LIMIT = 56 * 1024 * 1024


def nt(left, right):
    return lax.dot_general(left, right, (((1,), (1,)), ((), ())), preferred_element_type=F32)


def nn(left, right):
    return lax.dot_general(left, right, (((1,), (0,)), ((), ())), preferred_element_type=F32)


def segments(marks_ref):
    tok = marks_ref.shape[1]
    row = lax.broadcasted_iota(jnp.int32, (tok, tok), 0)
    col = lax.broadcasted_iota(jnp.int32, (tok, tok), 1)
    lower = jnp.where(col <= row, 1.0, 0.0).astype(BF)
    marks = jnp.broadcast_to(jnp.where(marks_ref[...] == 1, 1.0, 0.0), (tok, tok)).astype(BF)
    return nt(lower, marks), nt(marks, lower), row, col


def identity(size):
    row = lax.broadcasted_iota(jnp.int32, (size, size), 0)
    col = lax.broadcasted_iota(jnp.int32, (size, size), 1)
    return jnp.where(row == col, 1.0, 0.0).astype(BF)


def reversal():
    row = lax.broadcasted_iota(jnp.int32, (TILE, TILE), 0)
    col = lax.broadcasted_iota(jnp.int32, (TILE, TILE), 1)
    return jnp.where(row + col == TILE - 1, 1.0, 0.0).astype(BF)


def fill_shifts(shift_ref, marks_ref, short, forward):
    seg_col, seg_row, row, col = segments(marks_ref)
    tok = marks_ref.shape[1]
    same = seg_col == seg_row
    for lag in range(short):
        hit = (row - col == lag) if forward else (col - row == lag)
        shift_ref[lag * tok : (lag + 1) * tok, :] = jnp.where(hit & same, 1.0, 0.0).astype(BF)


def feats_kernel(marks, x, w, tails, ups, feats, mixed_t, mixed_tail, gate_head, shifts):
    short = w.shape[1]
    tok = marks.shape[1]

    @pl.when(pl.program_id(0) == 0)
    def _():
        fill_shifts(shifts, marks, short, True)

    seg_col, seg_row, _, _ = segments(marks)
    block = x.shape[1]
    eye = identity(block)
    outs = []
    rows = []
    for j in range(3):
        moved = nt(shifts[...], x[j])
        total = w[j, 0:1, :] * moved[0:tok]
        for lag in range(1, short):
            total = total + w[j, lag : lag + 1, :] * moved[lag * tok : (lag + 1) * tok]
        pad = jnp.concatenate(
            [tails[j].astype(F32), jnp.zeros((EDGE_ROWS, block), F32)], axis=0
        )
        fix = jnp.zeros((EDGE_ROWS, block), F32)
        for lag in range(1, short):
            fix = fix + w[j, lag : lag + 1, :] * pad[EDGE_ROWS - lag : 2 * EDGE_ROWS - lag]
        head = total[0:EDGE_ROWS] + jnp.where(seg_col[0:EDGE_ROWS, 0:block] == 0, fix, 0.0)
        total = jnp.concatenate([head, total[EDGE_ROWS:]], axis=0).astype(BF)
        rows.append(total)
        outs.append(nt(eye, total))
        feats[j] = outs[j].astype(BF)
    product = (rows[1].astype(F32) * rows[2].astype(F32)).astype(BF)
    flip = reversal()
    for b in range(tok // TILE):
        span = slice(b * TILE, (b + 1) * TILE)
        mixed_t[span, :] = nn(flip, product[span]).astype(BF)
    mixed = outs[1][:, tok - TILE :] * outs[2][:, tok - TILE :]
    first = seg_row[0:1, :]
    open_end = first[:, tok - TILE :] == first[:, tok - 1 : tok]
    mixed_tail[...] = jnp.where(open_end, mixed, 0.0).astype(BF)
    gate = ups[...].astype(F32) * outs[0][:, 0:TILE]
    gate_head[...] = jnp.where(first[:, 0:TILE] == 0, gate, 0.0).astype(BF)


def circulant(filt, g):
    row = filt[g : g + 1, :].astype(BF).astype(F32)
    wide = jnp.broadcast_to(row, (TILE, TILE))
    return pltpu.roll(wide, 0, 1, stride=1, stride_axis=0).astype(BF)


def diagonals(product):
    moved = pltpu.roll(product, 1, 1, stride=1, stride_axis=0)
    return jnp.sum(moved, axis=0, keepdims=True)


def own_kernel(members, marks, feats, ups, mixed_t, filt, conv, back, part):
    seg_col, seg_row, row, col = segments(marks)
    block = feats.shape[1]
    masks = []
    masks_bf = []
    for b in range(2):
        lo = b * TILE
        span = slice(lo, lo + TILE)
        keep = (seg_col[span, span] == seg_row[span, span]) & (col[span, span] >= row[span, span])
        masks_bf.append(jnp.where(keep, 1.0, 0.0).astype(BF))
        masks.append(nn(reversal(), masks_bf[b]))
    mixed = (feats[1].astype(F32) * feats[2].astype(F32)).astype(BF)
    gate = (ups[...].astype(F32) * feats[0].astype(F32)).astype(BF)
    lane = lax.broadcasted_iota(jnp.int32, (TILE, TILE), 1)
    for g in range(block // members):
        table = circulant(filt, g)
        rows = slice(g * members, (g + 1) * members)
        cb = (g * members) // TILE
        mine = (lane >= g * members - cb * TILE) & (lane < (g + 1) * members - cb * TILE)
        mine_bf = jnp.where(mine, 1.0, 0.0).astype(BF)
        total = None
        for b in range(2):
            span = slice(b * TILE, (b + 1) * TILE)
            diag = table * masks_bf[b]
            conv[rows, span] = nn(mixed[rows, span], diag)
            back[rows, span] = nt(gate[rows, span], diag)
            chans = slice(cb * TILE, (cb + 1) * TILE)
            product = nn(mixed_t[span, chans] * mine_bf, gate[chans, span]) * masks[b]
            total = product if total is None else total + product
        part[g : g + 1, :] = diagonals(total)


def grads_kernel(
    members, marks, x, w, tails, feats, ups, mixed_t, mixed_halo, gate_halo, conv, back, filt, part,
    mixed_out, grads, heads, short_grad, filt_grad, shifts, conv_s, back_s,
):
    short = w.shape[1]
    tok = marks.shape[1]
    block = x.shape[1]

    @pl.when(pl.program_id(0) == 0)
    def _():
        fill_shifts(shifts, marks, short, False)

    seg_col, seg_row, row, col = segments(marks)
    eye = identity(block)
    first = seg_row[0:1, :]
    middle = first[:, TILE - 1 : TILE]
    last = first[:, tok - 1 : tok]
    from_start = [
        jnp.where(first[:, 0:TILE] == 0, 1.0, 0.0),
        jnp.where(first[:, TILE:] == middle, 1.0, 0.0),
    ]
    to_end = [
        jnp.where(first[:, 0:TILE] == middle, 1.0, 0.0),
        jnp.where(first[:, TILE:] == last, 1.0, 0.0),
    ]
    upper_bf = jnp.where(col[0:TILE, 0:TILE] < row[0:TILE, 0:TILE], 1.0, 0.0).astype(BF)
    upper = jnp.where(col[0:TILE, 0:TILE] + row[0:TILE, 0:TILE] < TILE - 1, 1.0, 0.0)
    fq = feats[0].astype(F32)
    fk = feats[1].astype(F32)
    fv = feats[2].astype(F32)
    up = ups[...].astype(F32)
    mixed0 = ((fk[:, 0:TILE] * fv[:, 0:TILE]) * to_end[0]).astype(BF)
    gate1 = ((up[:, TILE:] * fq[:, TILE:]) * from_start[1]).astype(BF)
    mixed_h = mixed_halo[...]
    gate_h = gate_halo[...]
    gate0 = ((up[:, 0:TILE] * fq[:, 0:TILE]) * from_start[0]).astype(BF)
    mixed_ht = nt(reversal(), mixed_h).astype(BF)
    keep_col = (seg_col[0:TILE, 0:TILE] == seg_col[TILE - 1 : TILE, 0:TILE])
    keep_bf = nn(reversal(), jnp.where(keep_col, 1.0, 0.0).astype(BF)).astype(BF)
    lane = lax.broadcasted_iota(jnp.int32, (TILE, TILE), 1)
    for g in range(block // members):
        table = circulant(filt, g) * upper_bf
        rows = slice(g * members, (g + 1) * members)
        cb = (g * members) // TILE
        chans = slice(cb * TILE, (cb + 1) * TILE)
        mine = (lane >= g * members - cb * TILE) & (lane < (g + 1) * members - cb * TILE)
        mine_bf = jnp.where(mine, 1.0, 0.0).astype(BF)
        ahead = nn(jnp.concatenate([mixed_h[rows], mixed0[rows]], axis=0), table)
        conv_s[rows, 0:TILE] = conv[rows, 0:TILE] + ahead[0:members] * from_start[0]
        conv_s[rows, TILE:] = conv[rows, TILE:] + ahead[members:] * from_start[1]
        behind = nt(jnp.concatenate([gate1[rows], gate_h[rows]], axis=0), table)
        back_s[rows, 0:TILE] = back[rows, 0:TILE] + behind[0:members] * to_end[0]
        back_s[rows, TILE:] = back[rows, TILE:] + behind[members:] * to_end[1]
        product = nn(mixed_ht[:, chans] * mine_bf, gate0[chans]) + nn(
            mixed_t[0:TILE, chans] * (keep_bf * mine_bf), gate1[chans]
        )
        filt_grad[g : g + 1, :] = part[g : g + 1, :] + diagonals(product * upper)
    conv_v = conv_s[...]
    back_v = back_s[...]
    mixed_out[...] = (fq * conv_v).astype(BF)
    feat_grad = [
        (up * conv_v).astype(BF),
        (back_v * fv).astype(BF),
        (back_v * fk).astype(BF),
    ]
    open_start = seg_col[0:EDGE_ROWS, 0:block] == 0
    for j in range(3):
        moved = nt(shifts[...], feat_grad[j])
        raw = nt(eye, x[j])
        head = jnp.where(open_start, moved[0:EDGE_ROWS], 0.0)
        heads[j] = head.astype(BF)
        pad = jnp.concatenate(
            [tails[j].astype(F32), jnp.zeros((EDGE_ROWS, block), F32)], axis=0
        )
        total = None
        sums = []
        for lag in range(short):
            piece = moved[lag * tok : (lag + 1) * tok]
            term = w[j, lag : lag + 1, :] * piece
            total = term if total is None else total + term
            column = jnp.sum(raw * piece, axis=0, keepdims=True)
            if lag > 0:
                cross = head * pad[EDGE_ROWS - lag : 2 * EDGE_ROWS - lag]
                column = column + jnp.sum(cross, axis=0, keepdims=True)
            sums.append(column)
        sums.append(jnp.zeros((1, block), F32))
        stacked = jnp.concatenate(sums, axis=0)
        for h in range(block // TILE):
            short_grad[j, h] = stacked[:, h * TILE : (h + 1) * TILE]
        grads[j] = nt(eye, total.astype(BF)).astype(BF)


def fix_kernel(marks, w, next_heads, grads_in, grads):
    short = w.shape[1]
    tok = marks.shape[1]
    block = grads.shape[1]
    seg_col, _, _, _ = segments(marks)
    open_end = seg_col[tok - EDGE_ROWS :, 0:block] == seg_col[tok - 1 : tok, 0:block]
    eye = identity(block)
    for j in range(3):
        pad = jnp.concatenate(
            [jnp.zeros((EDGE_ROWS, block), F32), next_heads[j].astype(F32)], axis=0
        )
        fix = jnp.zeros((EDGE_ROWS, block), F32)
        for lag in range(1, short):
            fix = fix + w[j, lag : lag + 1, :] * pad[lag : lag + EDGE_ROWS]
        fix = jnp.where(open_end, fix, 0.0)
        wide = jnp.concatenate([jnp.zeros((TILE - EDGE_ROWS, block), F32), fix], axis=0)
        grads[j] = (grads_in[j].astype(F32) + nt(eye, wide.astype(BF))).astype(BF)


def shapes(*items):
    return [jax.ShapeDtypeStruct(s, d) for s, d in items]


def params():
    return pltpu.CompilerParams(vmem_limit_bytes=LIMIT)


def step_forward(block, size):
    return lax.ppermute(block, SEQ, [(i, i + 1) for i in range(size - 1)])


def step_back(block, size):
    return lax.ppermute(block, SEQ, [(i + 1, i) for i in range(size - 1)])


def exchange(pieces, axes):
    return lax.all_to_all(pieces, axes, 0, 0)


def local(streams, short_taps, long_taps, doc_marks, upstream):
    chan, tok = streams.shape[1:]
    groups, taps = long_taps.shape
    short = short_taps.shape[2]
    members = chan // groups
    steps = chan // BLOCK
    per = BLOCK // members
    size = lax.axis_size(SEQ)
    w = jnp.transpose(short_taps, (0, 2, 1))
    marks = doc_marks.reshape(1, tok)

    late = doc_marks[tok - EDGE_ROWS :]
    spots = jnp.arange(EDGE_ROWS)
    blocked = jnp.sum(jnp.where(spots[None, :] > spots[:, None], late[None, :], 0), axis=1)
    open_tail = (blocked == 0).astype(BF)
    tails = step_forward(
        jnp.transpose(streams[:, :, tok - EDGE_ROWS :] * open_tail, (0, 2, 1)), size
    )

    one = pl.BlockSpec((1, tok), lambda i: (0, 0))
    three = pl.BlockSpec((3, BLOCK, tok), lambda i: (0, i, 0))
    wspec = pl.BlockSpec((3, short, BLOCK), lambda i: (0, 0, i))
    espec = pl.BlockSpec((3, EDGE_ROWS, BLOCK), lambda i: (0, 0, i))
    full = pl.BlockSpec((BLOCK, tok), lambda i: (i, 0))
    tile0 = pl.BlockSpec((BLOCK, TILE), lambda i: (i, 0))
    tspec = pl.BlockSpec((tok, BLOCK), lambda i: (0, i))
    fspec = pl.BlockSpec((per, taps), lambda i: (i, 0))

    feats, mixed_t, mixed_tail, gate_head = pl.pallas_call(
        feats_kernel,
        grid=(steps,),
        in_specs=[one, three, wspec, espec, tile0],
        out_specs=[three, tspec, tile0, tile0],
        out_shape=shapes(
            ((3, chan, tok), BF), ((tok, chan), BF), ((chan, TILE), BF), ((chan, TILE), BF)
        ),
        scratch_shapes=[pltpu.VMEM((short * tok, tok), BF)],
        compiler_params=params(),
    )(marks, streams, w, tails, upstream)
    mixed_halo = step_forward(mixed_tail, size)
    gate_halo = step_back(gate_head, size)

    conv, back, part = pl.pallas_call(
        functools.partial(own_kernel, members),
        grid=(steps,),
        in_specs=[one, three, full, tspec, fspec],
        out_specs=[full, full, fspec],
        out_shape=shapes(((chan, tok), F32), ((chan, tok), F32), ((groups, taps), F32)),
        compiler_params=params(),
        cost_estimate=pl.CostEstimate(flops=2 * 10**9, bytes_accessed=8 * 10**6, transcendentals=0),
    )(marks, feats, upstream, mixed_t, long_taps)

    mixed_out, grads, heads, short_part, filt_part = pl.pallas_call(
        functools.partial(grads_kernel, members),
        grid=(steps,),
        in_specs=[
            one, three, wspec, espec, three, full, tspec, tile0, tile0, full, full, fspec, fspec
        ],
        out_specs=[
            full, three, espec,
            pl.BlockSpec((3, BLOCK // TILE, EDGE_ROWS, TILE), lambda i: (0, i, 0, 0)),
            fspec,
        ],
        out_shape=shapes(
            ((chan, tok), BF), ((3, chan, tok), BF), ((3, EDGE_ROWS, chan), BF),
            ((3, chan // TILE, EDGE_ROWS, TILE), F32), ((groups, taps), F32),
        ),
        scratch_shapes=[
            pltpu.VMEM((short * tok, tok), BF),
            pltpu.VMEM((BLOCK, tok), F32),
            pltpu.VMEM((BLOCK, tok), F32),
        ],
        compiler_params=params(),
    )(
        marks, streams, w, tails, feats, upstream, mixed_t, mixed_halo, gate_halo, conv, back,
        long_taps, part,
    )
    next_heads = step_back(heads, size)

    cube = lax.axis_size(CUBE)
    rest = lax.axis_size("zh")
    tp = lax.axis_size(TP)
    flat = jnp.concatenate([filt_part, short_part.reshape(-1, TILE)], axis=0)
    share = flat.shape[0] // cube
    mine = jnp.sum(exchange(flat.reshape(cube, share, TILE), CUBE), axis=0)
    mine = jnp.sum(exchange(jnp.broadcast_to(mine, (rest,) + mine.shape), "zh"), axis=0)
    total = exchange(jnp.broadcast_to(mine, (cube,) + mine.shape), CUBE).reshape(flat.shape)
    square = jnp.sum(total * total)
    squares = exchange(jnp.broadcast_to(square, (tp, EDGE_ROWS, TILE)), TP)
    entries = tp * (groups * taps + 3 * chan * short)
    mean = jnp.sum(squares[:, 0, 0]) / entries
    scale = jnp.minimum(1.0, 1.0 / jnp.sqrt(mean + 1e-06))

    last = pl.BlockSpec((3, BLOCK, TILE), lambda i: (0, i, tok // TILE - 1))
    grads = pl.pallas_call(
        fix_kernel,
        grid=(steps,),
        in_specs=[one, wspec, espec, last],
        out_specs=last,
        out_shape=jax.ShapeDtypeStruct(grads.shape, BF),
        input_output_aliases={3: 0},
        compiler_params=params(),
    )(marks, w, next_heads, grads)
    total = total * scale
    grad_long = total[0:groups]
    grad_short = total[groups:].reshape(3, chan // TILE, EDGE_ROWS, TILE)[:, :, 0:short]
    grad_short = jnp.transpose(grad_short, (0, 1, 3, 2)).reshape(3, chan, short)
    return (mixed_out, grads, grad_long, grad_short)


def solution(mesh):
    fine = Mesh(mesh.devices.reshape(4, 4, 4, 4, 2), ("x", "zh", "zl", "y", "c"))
    in_specs = (P(None, TP, SEQ), P(None, TP, None), P(TP, None), P(SEQ), P(TP, SEQ))
    out_specs = (P(TP, SEQ), P(None, TP, SEQ), P(TP, None), P(None, TP, None))
    return jax.shard_map(local, mesh=fine, in_specs=in_specs, out_specs=out_specs, check_vma=False)
```

time: 506 us -> 125 us (0.25)
  blocking collectives: 281 us -> 40.3 us
  local copies, waits for them, and re-layouts: 96.3 us -> 7.6 us
  other arithmetic: 58.7 us -> 2.38 us
  Pallas kernels: 0 us -> 40.4 us
  waiting for transfers between devices: 23.1 us -> 7.17 us
  between operations: 16.6 us -> 1.44 us
  matrix products: 9.96 us -> 0 us
  starting transfers between devices: 16.8 us -> 24.8 us
    psum x2 -> x0, blocking collectives: 281 us -> none  [the longest x1 230 us: local(): filt_total, short_total = lax.psum((filt_grad, short_grad), 'seq')]
    pallas_call x0 -> x4, Pallas kernels: none -> 40.4 us  [the longest x1 15.9 us: local(): pl.pallas_call(functools.partial(grads_kernel, members), grid=(steps,), i...]
    all_to_all x0 -> x2, blocking collectives: none -> 40.3 us  [exchange(): return lax.all_to_all(pieces, axes, 0, 0)]
    reshape x9 -> x1, local copies, waits for them, and re-layouts: 29.7 us -> 0.65 us  [local(): grad_short = jnp.transpose(grad_short, (0, 1, 3, 2)).reshape(3, chan, short)]
    convert_element_type x11 -> x1, other arithmetic: 23.8 us -> 0.01 us  [local(): open_tail = (blocked == 0).astype(BF)]
    psum x1 -> x0, waiting for transfers between devices: 19.8 us -> none  [local(): filt_total, short_total = lax.psum((filt_grad, short_grad), 'seq')]
    another operation x24 -> x0, local copies, waits for them, and re-layouts: 16.3 us -> none  [the longest x16 16 us: band_table(): tiled = jnp.tile(base, (1, rows))[:, :rows * width]]
    all_to_all x0 -> x2, starting transfers between devices: none -> 14.2 us  [exchange(): return lax.all_to_all(pieces, axes, 0, 0)]
  transfers between devices with their start and end apart: 7 -> 6, of which waited for: 2 -> 2; matrix products, arithmetic and copies ran while one was open for 5% -> 2% of each run, Pallas kernels for 0% -> 11%
where the time goes in v1:
time: 125 us; the launch traced here: 124 us
  Pallas kernels  40.4 us (32%)
  blocking collectives  40.3 us (32%)
  starting transfers between devices  24.8 us (20%)
  local copies, waits for them, and re-layouts  7.6 us (6%)
  waiting for transfers between devices  7.17 us (6%)
  other arithmetic  2.38 us (2%)
  between operations  1.44 us (1%)
    all_to_all x2, blocking collectives, exchange(): return lax.all_to_all(pieces, axes, 0, 0)  40.3 us
    pallas_call x1, Pallas kernels, local(): pl.pallas_call(functools.partial(grads_kernel, members), grid=(steps,), i...  15.9 us
    all_to_all x2, starting transfers between devices, exchange(): return lax.all_to_all(pieces, axes, 0, 0)  14.2 us
    pallas_call x1, Pallas kernels, local(): pl.pallas_call(feats_kernel, grid=(steps,), in_specs=[one, three, wspec,...  11.1 us
    pallas_call x1, Pallas kernels, local(): pl.pallas_call(functools.partial(own_kernel, members), grid=(steps,), in_...  8.98 us
    ppermute x2, starting transfers between devices, step_forward(): return lax.ppermute(block, SEQ, [(i, i + 1) for i in range(size - 1)])  8.05 us
    all_to_all x2, waiting for transfers between devices, exchange(): return lax.all_to_all(pieces, axes, 0, 0)  6 us
    pallas_call x1, Pallas kernels, local(): pl.pallas_call(fix_kernel, grid=(steps,), in_specs=[one, wspec, espec, la...  4.38 us
  transfers between devices with their start and end apart: 6, of which 2 were waited for; matrix products, arithmetic and copies ran while one was open for 2% of the time, Pallas kernels for 11%

profile of v1, /device:TPU:1, one launch (start us, length us, event | category | flops | bytes accessed | tf_op | source)
XLA Modules:
  0.0 124.0 jit_solution(13446574054614153076)
XLA Ops:
  0.6 0.8 slice.23
  1.4 0.1 select_reduce_fusion
  1.5 1.4 %slice.22 = bf16[3,1024,8]{2,1,0:T(8,128)(2,1)S(1)} slice(bf16[3,1024,256]{2,1,0:T(8,128)(2,1)} %x.3), slice={[0:3], [0:1024], [248:256]} | slice | bytes 98304 | tf_op jit(solution)/shard_map/slice | solution.py:292
  2.9 0.2 copy.16
  3.2 0.1 multiply_bitcast_fusion
  3.2 4.4 %collective-permute-start = (bf16[3,8,1024]{2,1,0:T(8,128)(2,1)S(1)}, bf16[3,8,1024]{2,1,0:T(8,128)(2,1)S(1)}, u32[]{:S(2)}, u32[]{:S(2)}) collective-permute-start(bf16[3,8,1024]{2,1,0:T(8,128)(2,1)S(1)} %multiply_bitcast_fusion), channel_id=1, source_target_pairs={{0,8},{8,16},{16,24},{24,32},{32,40},{40,48},{48,56},{56,64},{64,7... | collective-permute-start | bytes 147464 | tf_op jit(solution)/shard_map/ppermute | solution.py:265
  7.6 1.2 collective-permute-done.tails
  8.8 0.0 copy-start.2
  8.8 0.6 copy-done.2
  9.4 11.1 %shard_map.84 = (bf16[3,1024,256]{2,1,0:T(8,128)(2,1)}, bf16[256,1024]{1,0:T(8,128)(2,1)}, bf16[1024,128]{1,0:T(8,128)(2,1)}, bf16[1024,128]{1,0:T(8,128)(2,1)}) custom-call(s32[1,256]{1,0:T(1,128)} %bitcast.19, bf16[3,1024,256]{2,1,0:T(8,128)(2,1)} %x.3, f32[3,7,1024]{2,1,0:T(8,128)} %bitcast.12, bf16[3,8,1024]{2,1,0:T(8,128)(2,1)} %copy-done.2, ...), custom_call_target="tpu_custom_call" | custom-call | tf_op jit(solution)/shard_map/pallas_call | solution.py:304
  20.5 3.7 %collective-permute-start.1 = (bf16[1024,128]{1,0:T(8,128)(2,1)}, bf16[1024,128]{1,0:T(8,128)(2,1)S(1)}, u32[]{:S(2)}, u32[]{:S(2)}) collective-permute-start(bf16[1024,128]{1,0:T(8,128)(2,1)} %get-tuple-element.18), channel_id=1, source_target_pairs={{0,8},{8,16},{16,24},{24,32},{32,40},{40,48},{48,56},{56,64},{64,7... | collective-permute-start | bytes 786440 | tf_op jit(solution)/shard_map/ppermute | solution.py:265
  24.2 1.3 %collective-permute-start.2 = (bf16[1024,128]{1,0:T(8,128)(2,1)}, bf16[1024,128]{1,0:T(8,128)(2,1)S(1)}, u32[]{:S(2)}, u32[]{:S(2)}) collective-permute-start(bf16[1024,128]{1,0:T(8,128)(2,1)} %get-tuple-element.19), channel_id=1, source_target_pairs={{8,0},{16,8},{24,16},{32,24},{40,32},{48,40},{56,48},{64,56},{72,6... | collective-permute-start | bytes 786440 | tf_op jit(solution)/shard_map/ppermute | solution.py:269
  25.5 9.0 %shard_map.85 = (f32[1024,256]{1,0:T(8,128)}, f32[1024,256]{1,0:T(8,128)}, f32[64,128]{1,0:T(8,128)}) custom-call(s32[1,256]{1,0:T(1,128)} %bitcast.20, bf16[3,1024,256]{2,1,0:T(8,128)(2,1)} %get-tuple-element.16.feats, bf16[1024,256]{1,0:T(8,128)(2,1)} %ups.5, bf16[256,1024]{1,0:T(8,128)(2,1)} %get-tuple-element.17.mixed_t, f32[64,128]{1,0:T(8,128)} %filt.3), custom_call_target="tpu_custom_call" | custom-call | flops 2000000000 | bytes 8000000 | tf_op jit(solution)/shard_map/pallas_call | solution.py:318
  34.5 0.0 collective-permute-done.1.mixed_halo
  34.5 0.0 copy-start
  34.5 0.0 collective-permute-done.2.gate_halo
  34.5 0.0 copy-start.1
  34.5 0.7 copy-done
  35.2 0.1 copy-done.1
  35.3 15.9 %shard_map.86 = (bf16[1024,256]{1,0:T(8,128)(2,1)}, bf16[3,1024,256]{2,1,0:T(8,128)(2,1)}, bf16[3,8,1024]{2,1,0:T(8,128)(2,1)}, f32[3,8,8,128]{3,2,1,0:T(8,128)}, f32[64,128]{1,0:T(8,128)}) custom-call(s32[1,256]{1,0:T(1,128)} %bitcast.21, bf16[3,1024,256]{2,1,0:T(8,128)(2,1)} %x.3, f32[3,7,1024]{2,1,0:T(8,128)} %bitcast.13, bf16[3,8,1024]{2,1,0:T(8,128)(2,1)} %copy-done.2, ...), custom_call_target="tpu_custom_call" | custom-call | tf_op jit(solution)/shard_map/pallas_call | solution.py:328
  51.2 0.9 pad_maximum_fusion
  52.1 21.5 %all_to_all.20 = f32[16,16,128]{2,1,0:T(8,128)S(1)} all-to-all(f32[16,16,128]{2,1,0:T(8,128)S(1)} %bitcast.15), channel_id=1, replica_groups=mesh['x'=4,'zh'=4,'zl'=4,'y'=4,'c'=2] {'x','zl'}, dimensions={0} | all-to-all | bytes 262144 | tf_op jit(solution)/shard_map/all_to_all | solution.py:273
  73.6 18.8 %all_to_all.21 = f32[4,16,128]{2,1,0:T(8,128)S(1)} all-to-all(f32[4,16,128]{2,1,0:T(8,128)S(1)} %broadcast_in_dim.27), channel_id=1, replica_groups=mesh['x'=4,'zh'=4,'zl'=4,'y'=4,'c'=2] {'zh'}, dimensions={0} | all-to-all | bytes 65536 | tf_op jit(solution)/shard_map/all_to_all | solution.py:273
  92.4 0.7 broadcast_in_dim.28
  93.0 3.5 %all-to-all-start.2 = ((f32[16,16,128]{2,1,0:T(8,128)}), f32[16,16,128]{2,1,0:T(8,128)S(1)}, u32[]{:S(2)}, u32[]{:S(2)}) async-start(f32[16,16,128]{2,1,0:T(8,128)} %broadcast_in_dim.28), calls=%async_computation.2 | async-start | bytes 262144 | tf_op jit(solution)/shard_map/all_to_all | solution.py:273
  96.6 1.3 %collective-permute-start.3 = (bf16[3,8,1024]{2,1,0:T(8,128)(2,1)}, bf16[3,8,1024]{2,1,0:T(8,128)(2,1)S(1)}, u32[]{:S(2)}, u32[]{:S(2)}) collective-permute-start(bf16[3,8,1024]{2,1,0:T(8,128)(2,1)} %get-tuple-element.24), channel_id=1, source_target_pairs={{8,0},{16,8},{24,16},{32,24},{40,32},{48,40},{56,48},{64,56},{72,6... | collective-permute-start | bytes 147464 | tf_op jit(solution)/shard_map/ppermute | solution.py:269
  97.9 6.0 %all-to-all-done.2 = f32[16,16,128]{2,1,0:T(8,128)S(1)} async-done(((f32[16,16,128]{2,1,0:T(8,128)}), f32[16,16,128]{2,1,0:T(8,128)S(1)}, u32[]{:S(2)}, u32[]{:S(2)}) %all-to-all-start.2) | async-done | bytes 131104 | tf_op jit(solution)/shard_map/all_to_all | solution.py:273
  103.9 0.6 multiply_reduce_fusion
  104.5 1.3 %broadcast_in_dim.29 = f32[8,8,128]{2,1,0:T(8,128)} broadcast(f32[]{:T(128)} %multiply_reduce_fusion), dimensions={} | broadcast | bytes 32772 | tf_op jit(solution)/shard_map/broadcast_in_dim | solution.py:364
  105.8 10.6 %all-to-all-start.3 = ((f32[8,8,128]{2,1,0:T(8,128)}), f32[8,8,128]{2,1,0:T(8,128)S(1)}, u32[]{:S(2)}, u32[]{:S(2)}) async-start(f32[8,8,128]{2,1,0:T(8,128)} %broadcast_in_dim.29), calls=%async_computation.3 | async-start | bytes 65536 | tf_op jit(solution)/shard_map/all_to_all | solution.py:273
  116.4 0.0 collective-permute-done.3.next_heads
  116.4 0.0 copy-start.3
  116.4 0.6 copy-done.3
  117.0 4.4 %shard_map.87 = bf16[3,1024,256]{2,1,0:T(8,128)(2,1)} custom-call(s32[1,256]{1,0:T(1,128)} %bitcast.22, f32[3,7,1024]{2,1,0:T(8,128)} %bitcast.14, bf16[3,8,1024]{2,1,0:T(8,128)(2,1)} %copy-done.3, bf16[3,1024,256]{2,1,0:T(8,128)(2,1)} %get-tuple-element.25.grads_in), custom_call_target="tpu_custom_call", output_to_operand_aliasing={{}: (3, {})} | custom-call | tf_op jit(solution)/shard_map/pallas_call | solution.py:370
  121.4 0.0 all-to-all-done.3
  121.4 0.6 slice_reduce_fusion
  122.7 0.6 slice.30
  123.4 0.6 slice_bitcast_fusion
  (6 shorter events, 0.1 us)
Async XLA Ops:
  3.2 5.5 %collective-permute-start = (bf16[3,8,1024]{2,1,0:T(8,128)(2,1)S(1)}, bf16[3,8,1024]{2,1,0:T(8,128)(2,1)S(1)}, u32[]{:S(2)}, u32[]{:S(2)}) collective-permute-start(bf16[3,8,1024]{2,1,0:T(8,128)(2,1)S(1)} %multiply_bitcast_fusion), channel_id=1, source_target_pairs={{0,8},{8,16},{16,24},{24,32},{32,40},{40,48},{48,56},{56,64},{64,7... | collective-permute-start | bytes 147464 | tf_op jit(solution)/shard_map/ppermute | solution.py:265
  8.8 0.6 copy-start.2
  20.5 14.0 %collective-permute-start.1 = (bf16[1024,128]{1,0:T(8,128)(2,1)}, bf16[1024,128]{1,0:T(8,128)(2,1)S(1)}, u32[]{:S(2)}, u32[]{:S(2)}) collective-permute-start(bf16[1024,128]{1,0:T(8,128)(2,1)} %get-tuple-element.18), channel_id=1, source_target_pairs={{0,8},{8,16},{16,24},{24,32},{32,40},{40,48},{48,56},{56,64},{64,7... | collective-permute-start | bytes 786440 | tf_op jit(solution)/shard_map/ppermute | solution.py:265
  24.2 10.3 %collective-permute-start.2 = (bf16[1024,128]{1,0:T(8,128)(2,1)}, bf16[1024,128]{1,0:T(8,128)(2,1)S(1)}, u32[]{:S(2)}, u32[]{:S(2)}) collective-permute-start(bf16[1024,128]{1,0:T(8,128)(2,1)} %get-tuple-element.19), channel_id=1, source_target_pairs={{8,0},{16,8},{24,16},{32,24},{40,32},{48,40},{56,48},{64,56},{72,6... | collective-permute-start | bytes 786440 | tf_op jit(solution)/shard_map/ppermute | solution.py:269
  34.5 0.7 copy-start
  34.5 0.8 copy-start.1
  93.0 10.8 %all-to-all-start.2 = ((f32[16,16,128]{2,1,0:T(8,128)}), f32[16,16,128]{2,1,0:T(8,128)S(1)}, u32[]{:S(2)}, u32[]{:S(2)}) async-start(f32[16,16,128]{2,1,0:T(8,128)} %broadcast_in_dim.28), calls=%async_computation.2 | async-start | bytes 262144 | tf_op jit(solution)/shard_map/all_to_all | solution.py:273
  96.6 19.8 %collective-permute-start.3 = (bf16[3,8,1024]{2,1,0:T(8,128)(2,1)}, bf16[3,8,1024]{2,1,0:T(8,128)(2,1)S(1)}, u32[]{:S(2)}, u32[]{:S(2)}) collective-permute-start(bf16[3,8,1024]{2,1,0:T(8,128)(2,1)} %get-tuple-element.24), channel_id=1, source_target_pairs={{8,0},{16,8},{24,16},{32,24},{40,32},{48,40},{56,48},{64,56},{72,6... | collective-permute-start | bytes 147464 | tf_op jit(solution)/shard_map/ppermute | solution.py:269
  105.8 15.7 %all-to-all-start.3 = ((f32[8,8,128]{2,1,0:T(8,128)}), f32[8,8,128]{2,1,0:T(8,128)S(1)}, u32[]{:S(2)}, u32[]{:S(2)}) async-start(f32[8,8,128]{2,1,0:T(8,128)} %broadcast_in_dim.29), calls=%async_computation.3 | async-start | bytes 65536 | tf_op jit(solution)/shard_map/all_to_all | solution.py:273
  116.4 0.6 copy-start.3

commit v2 on v0

v2 whole, which is shorter than its diff:
```python
import functools

import jax
import jax.numpy as jnp
from jax import lax
from jax.experimental import pallas as pl
from jax.experimental.pallas import tpu as pltpu
from jax.sharding import Mesh
from jax.sharding import PartitionSpec as P

BF = jnp.bfloat16
F32 = jnp.float32
SEQ = ("x", "zh", "zl")
TP = ("y", "c")
CUBE = ("x", "zl")
TILE = 128
EDGE = 8
PACK = 16
BLOCK = 256
LIMIT = 24 * 1024 * 1024
FIRST_LIMIT = 57 * 1024 * 1024


def nt(left, right):
    return lax.dot_general(left, right, (((1,), (1,)), ((), ())), preferred_element_type=F32)


def nn(left, right):
    return lax.dot_general(left, right, (((1,), (0,)), ((), ())), preferred_element_type=F32)


def ones_where(keep):
    return jnp.where(keep, 1.0, 0.0).astype(BF)


def grid_of(rows, cols):
    return (
        lax.broadcasted_iota(jnp.int32, (rows, cols), 0),
        lax.broadcasted_iota(jnp.int32, (rows, cols), 1),
    )


def segments(marks):
    tok = marks.shape[1]
    row, col = grid_of(tok, tok)
    lower = ones_where(col <= row)
    wide = jnp.broadcast_to(jnp.where(marks[...] == 1, 1.0, 0.0), (tok, tok)).astype(BF)
    return nt(lower, wide), nt(wide, lower), row, col


def identity(size):
    row, col = grid_of(size, size)
    return ones_where(row == col)


def reversal():
    row, col = grid_of(TILE, TILE)
    return ones_where(row + col == TILE - 1)


def fill_shifts(shifts, same, offset, short):
    tok = same.shape[0]
    for lag in range(short):
        shifts[lag * tok : (lag + 1) * tok, :] = ones_where((offset == lag) & same)


def tap_columns(w, j, span):
    short = w.shape[1]
    wide = jnp.concatenate(
        [w[j, :, span], jnp.zeros((EDGE - short, BLOCK), F32)], axis=0
    )
    return jnp.transpose(wide)


def weighted(values, taps, short):
    parts = []
    values = values.astype(F32)
    for lag in range(short):
        tap = jnp.broadcast_to(taps[:, lag : lag + 1], (BLOCK, TILE))
        for lo in range(0, values.shape[1], TILE):
            parts.append((values[:, lo : lo + TILE] * tap).astype(BF))
    return jnp.concatenate(parts, axis=1)


def edge_rows(packed, first, j, lo):
    rows = []
    for tile in range(lo // TILE, (lo + BLOCK) // TILE):
        at = first + (2 * tile + j // 2) * PACK
        rows.append(packed[at : at + PACK, :].astype(F32)[(j % 2) * EDGE : (j % 2 + 1) * EDGE])
    return jnp.concatenate(rows, axis=1)


def border_sum(w, j, span, pad, forward):
    total = None
    for lag in range(1, w.shape[1]):
        lo = EDGE - lag if forward else lag
        term = w[j, lag : lag + 1, span] * pad[lo : lo + EDGE]
        total = term if total is None else total + term
    return total


def after(rows):
    return jnp.concatenate([rows, jnp.zeros_like(rows)], axis=0)


def at_front(rows, eye):
    wide = jnp.concatenate([rows, jnp.zeros((TILE - EDGE, rows.shape[1]), F32)], axis=0)
    return nt(eye, wide.astype(BF))


def feats_kernel(marks, x, w, ups, feats, next_pack, last_pack, shifts):
    short = w.shape[1]
    chan, tok = ups.shape
    seg_col, seg_row, row, col = segments(marks)
    fill_shifts(shifts, seg_col == seg_row, col - row, short)
    first = seg_row[0:1, :]
    open_end = first == first[:, tok - 1 : tok]
    open_start = first == 0
    head_row, head_col = grid_of(PACK, tok)
    take_tail = ones_where((head_col == tok - EDGE + head_row) & open_end & (head_row < EDGE))
    take_head = ones_where((head_col == head_row) & (head_row < EDGE) & open_start)
    for lo in range(0, chan, BLOCK):
        span = slice(lo, lo + BLOCK)
        outs = []
        tails = []
        for j in range(3):
            raw = x[j, span]
            taps = tap_columns(w, j, span)
            out = nn(weighted(raw, taps, short), shifts[...]).astype(BF)
            feats[j, span] = out
            outs.append(out.astype(F32))
            tails.append(nt(take_tail, raw)[0:EDGE])
        tails.append(jnp.zeros_like(tails[0]))
        mixed = outs[1][:, tok - TILE :] * outs[2][:, tok - TILE :]
        next_pack[span, :] = jnp.where(open_end[:, tok - TILE :], mixed, 0.0).astype(BF)
        up = ups[span]
        gate = up[:, 0:TILE].astype(F32) * outs[0][:, 0:TILE]
        last_pack[span, :] = jnp.where(open_start[:, 0:TILE], gate, 0.0).astype(BF)
        heads = nt(take_head, up).astype(BF)
        pairs = [
            jnp.concatenate([tails[p], tails[p + 1]], axis=0).astype(BF) for p in (0, 2)
        ]
        for h in range(0, BLOCK, TILE):
            tile = (lo + h) // TILE
            at = chan + tile * PACK
            last_pack[at : at + PACK, :] = heads[:, h : h + TILE]
            for p in range(2):
                at = chan + (2 * tile + p) * PACK
                next_pack[at : at + PACK, :] = pairs[p][:, h : h + TILE]


def circulant(filt, g):
    row = filt[g : g + 1, :].astype(BF).astype(F32)
    wide = jnp.broadcast_to(row, (TILE, TILE))
    return pltpu.roll(wide, 0, 1, stride=1, stride_axis=0).astype(BF)


def diagonals(product):
    moved = pltpu.roll(product, 1, 1, stride=1, stride_axis=0)
    return jnp.sum(moved, axis=0, keepdims=True)


def members_mask(start, members):
    row, col = grid_of(TILE, TILE)
    return ones_where((col >= start) & (col < start + members))


def own_kernel(members, marks, feats, ups, filt, conv, back, part):
    chan, tok = ups.shape
    seg_col, seg_row, row, col = segments(marks)
    flip = reversal()
    s = slice(TILE, tok)
    keep_bf = ones_where((seg_col[s, s] == seg_row[s, s]) & (col[s, s] >= row[s, s]))
    keep = nn(flip, keep_bf)
    picks = [members_mask(p, members) for p in range(0, TILE, members)]
    for lo in range(0, chan, BLOCK):
        span = slice(lo, lo + BLOCK)
        mixed = (feats[1, span, s].astype(F32) * feats[2, span, s].astype(F32)).astype(BF)
        gate = (ups[span, s].astype(F32) * feats[0, span, s].astype(F32)).astype(BF)
        mixed_t = nt(flip, mixed).astype(BF)
        for g in range(BLOCK // members):
            n = lo // members + g
            table = circulant(filt, n) * keep_bf
            rows = slice(g * members, (g + 1) * members)
            at = slice(lo + g * members, lo + (g + 1) * members)
            cb = (g * members) // TILE
            chans = slice(cb * TILE, (cb + 1) * TILE)
            conv[at, :] = nn(mixed[rows], table)
            back[at, :] = nt(gate[rows], table)
            product = nn(mixed_t[:, chans] * picks[g % len(picks)], gate[chans])
            part[n : n + 1, :] = diagonals(product * keep)


def halo_kernel(
    members, marks, x, w, feats, ups, from_last, from_next, conv, back, filt, part, shifts,
    mixed_out, grads, heads, sums, conv_s, back_s,
):
    short = w.shape[1]
    chan, tok = ups.shape
    seg_col, seg_row, row, col = segments(marks)
    eye = identity(BLOCK)
    flip = reversal()
    first = seg_row[0:1, :]
    middle = first[:, TILE - 1 : TILE]
    last = first[:, tok - 1 : tok]
    from_start = [
        jnp.where(first[:, 0:TILE] == 0, 1.0, 0.0),
        jnp.where(first[:, TILE:] == middle, 1.0, 0.0),
    ]
    to_end = [
        jnp.where(first[:, 0:TILE] == middle, 1.0, 0.0),
        jnp.where(first[:, TILE:] == last, 1.0, 0.0),
    ]
    row_t, col_t = grid_of(TILE, TILE)
    upper_bf = ones_where(col_t < row_t)
    upper = jnp.where(col_t + row_t < TILE - 1, 1.0, 0.0)
    s = slice(0, TILE)
    keep_bf = ones_where((seg_col[s, s] == seg_row[s, s]) & (col[s, s] >= row[s, s]))
    keep = nn(flip, keep_bf)
    open_start = seg_col[0:EDGE, 0:BLOCK] == 0
    head_row, head_col = grid_of(EDGE, tok)
    take_head = ones_where((head_col == head_row) & (first == 0))
    take_tail = ones_where((head_col == tok - EDGE + head_row) & (first == last))
    picks = [members_mask(p, members) for p in range(0, TILE, members)]
    per = BLOCK // members
    stride = per + 3 * (BLOCK // TILE) * EDGE
    for lo in range(0, chan, BLOCK):
        span = slice(lo, lo + BLOCK)
        pads = [after(edge_rows(from_last, chan, j, lo)) for j in range(3)]
        feat = []
        for j in range(3):
            fix = jnp.where(open_start, border_sum(w, j, span, pads[j], True), 0.0)
            head = (feats[j, span, 0:TILE].astype(F32) + at_front(fix, eye)).astype(BF)
            feat.append(jnp.concatenate([head, feats[j, span, TILE:]], axis=1).astype(F32))
        up = ups[span].astype(F32)
        gate = up * feat[0]
        mixed = feat[1][:, 0:TILE] * feat[2][:, 0:TILE]
        mixed_b = mixed.astype(BF)
        gate_b = gate[:, 0:TILE].astype(BF)
        mixed0 = (mixed * to_end[0]).astype(BF)
        gate0 = (gate[:, 0:TILE] * from_start[0]).astype(BF)
        gate1 = (gate[:, TILE:] * from_start[1]).astype(BF)
        mixed_h = from_last[span]
        beyond = border_sum(w, 0, span, after(nt(take_tail, x[0, span])), True)
        ups_head = jnp.concatenate(
            [
                from_next[at : at + PACK, :].astype(F32)[0:EDGE]
                for at in range(chan + lo // TILE * PACK, chan + (lo + BLOCK) // TILE * PACK, PACK)
            ],
            axis=1,
        )
        gate_h = (from_next[span].astype(F32) + at_front(ups_head * beyond, eye)).astype(BF)
        lead_t = nt(flip, mixed_h).astype(BF)
        mixed_t = nt(flip, mixed0).astype(BF)
        whole_t = nt(flip, mixed_b).astype(BF)
        base = lo // BLOCK * stride
        for g in range(per):
            n = lo // members + g
            table = circulant(filt, n)
            diag = table * keep_bf
            table = table * upper_bf
            rows = slice(g * members, (g + 1) * members)
            at = slice(lo + g * members, lo + (g + 1) * members)
            cb = (g * members) // TILE
            chans = slice(cb * TILE, (cb + 1) * TILE)
            pick = picks[g % len(picks)]
            ahead = nn(jnp.concatenate([mixed_h[rows], mixed0[rows]], axis=0), table)
            conv_s[rows, 0:TILE] = nn(mixed_b[rows], diag) + ahead[0:members] * from_start[0]
            conv_s[rows, TILE:] = conv[at] + ahead[members:] * from_start[1]
            behind = nt(jnp.concatenate([gate1[rows], gate_h[rows]], axis=0), table)
            back_s[rows, 0:TILE] = nt(gate_b[rows], diag) + behind[0:members] * to_end[0]
            back_s[rows, TILE:] = back[at] + behind[members:] * to_end[1]
            product = nn(lead_t[:, chans] * pick, gate0[chans]) + nn(
                mixed_t[:, chans] * pick, gate1[chans]
            )
            inner = nn(whole_t[:, chans] * pick, gate_b[chans])
            sums[base + g : base + g + 1, :] = part[n : n + 1, :] + diagonals(
                product * upper + inner * keep
            )
        conv_v = conv_s[...]
        back_v = back_s[...]
        mixed_out[span, :] = (feat[0] * conv_v).astype(BF)
        grad = [
            (up * conv_v).astype(BF),
            (back_v * feat[2]).astype(BF),
            (back_v * feat[1]).astype(BF),
        ]
        for j in range(3):
            grads[j, span] = grad[j]
            moved = nt(shifts[...], grad[j])
            raw = nt(eye, x[j, span])
            head = nt(take_head, grad[j])
            heads[j, :, span] = head.astype(BF)
            columns = []
            for lag in range(short):
                piece = moved[lag * tok : (lag + 1) * tok]
                column = jnp.sum(raw * piece, axis=0, keepdims=True)
                if lag > 0:
                    cross = head * pads[j][EDGE - lag : 2 * EDGE - lag]
                    column = column + jnp.sum(cross, axis=0, keepdims=True)
                columns.append(column)
            columns += [jnp.zeros((1, BLOCK), F32)] * (EDGE - short)
            stacked = jnp.concatenate(columns, axis=0)
            for h in range(BLOCK // TILE):
                at = base + per + (j * (BLOCK // TILE) + h) * EDGE
                sums[at : at + EDGE, :] = stacked[:, h * TILE : (h + 1) * TILE]


def streams_kernel(marks, w, grads, next_heads, out, shifts):
    short = w.shape[1]
    tok = marks.shape[1]
    seg_col, seg_row, row, col = segments(marks)
    fill_shifts(shifts, seg_col == seg_row, row - col, short)
    open_end = seg_col[tok - EDGE :, 0:BLOCK] == seg_col[tok - 1 : tok, 0:BLOCK]
    eye = identity(BLOCK)
    for lo in range(0, grads.shape[1], BLOCK):
        span = slice(lo, lo + BLOCK)
        for j in range(3):
            taps = tap_columns(w, j, span)
            total = nn(weighted(grads[j, span], taps, short), shifts[...])
            pad = next_heads[j, :, span].astype(F32)
            pad = jnp.concatenate([jnp.zeros_like(pad), pad], axis=0)
            fix = jnp.where(open_end, border_sum(w, j, span, pad, False), 0.0)
            wide = jnp.concatenate([jnp.zeros((TILE - EDGE, BLOCK), F32), fix], axis=0)
            out[j, span, 0:TILE] = total[:, 0:TILE].astype(BF)
            out[j, span, TILE:] = (total[:, TILE:] + nt(eye, wide.astype(BF))).astype(BF)


def squares_kernel(total, out):
    value = total[...]
    out[...] = jnp.broadcast_to(jnp.sum(value * value), out.shape)


def scale_kernel(entries, total, squares, grad_long, grad_short):
    mean = jnp.sum(squares[:, 0, 0:1]) / entries
    wide = jnp.broadcast_to(mean, (EDGE, TILE))
    scale = jnp.minimum(1.0, 1.0 / jnp.sqrt(wide + 1e-06))[0:1]
    short = grad_short.shape[1]
    members = grad_short.shape[2] // grad_long.shape[0]
    per = BLOCK // members
    stride = per + 3 * (BLOCK // TILE) * EDGE
    for b in range(grad_short.shape[2] // BLOCK):
        base = b * stride
        grad_long[b * per : (b + 1) * per, :] = total[base : base + per, :] * scale
        for j in range(3):
            for h in range(BLOCK // TILE):
                at = base + per + (j * (BLOCK // TILE) + h) * EDGE
                lane = b * BLOCK + h * TILE
                grad_short[j, :, lane : lane + TILE] = total[at : at + short, :] * scale


def call(kernel, outs, scratch, *args, limit=LIMIT):
    return pl.pallas_call(
        kernel,
        in_specs=[pl.BlockSpec(memory_space=pltpu.VMEM) for _ in args],
        out_specs=[pl.BlockSpec(memory_space=pltpu.VMEM) for _ in outs],
        out_shape=[jax.ShapeDtypeStruct(s, d) for s, d in outs],
        scratch_shapes=scratch,
        compiler_params=pltpu.CompilerParams(vmem_limit_bytes=limit),
        cost_estimate=pl.CostEstimate(
            flops=2 * 10**9, bytes_accessed=8 * 10**6, transcendentals=0
        ),
    )(*args)


def step_forward(block, size):
    return lax.ppermute(block, SEQ, [(i, i + 1) for i in range(size - 1)])


def step_back(block, size):
    return lax.ppermute(block, SEQ, [(i + 1, i) for i in range(size - 1)])


def exchange(pieces, axes):
    return lax.all_to_all(pieces, axes, 0, 0)


def local(streams, short_taps, long_taps, doc_marks, upstream):
    chan, tok = streams.shape[1:]
    groups, taps = long_taps.shape
    short = short_taps.shape[2]
    members = chan // groups
    size = lax.axis_size(SEQ)
    w = jnp.transpose(short_taps, (0, 2, 1))
    marks = doc_marks.reshape(1, tok)
    shifts = ((short * tok, tok), BF)
    whole = ((3, chan, tok), BF)
    tiles = chan // TILE

    feats, next_pack, last_pack, moves = call(
        feats_kernel,
        [
            whole, ((chan + 2 * tiles * PACK, TILE), BF), ((chan + tiles * PACK, TILE), BF),
            shifts,
        ],
        [],
        marks, streams, w, upstream,
        limit=FIRST_LIMIT,
    )
    from_last = step_forward(next_pack, size)
    from_next = step_back(last_pack, size)

    half = ((chan, TILE), F32)
    conv, back, part = call(
        functools.partial(own_kernel, members),
        [half, half, ((groups, taps), F32)],
        [],
        marks, feats, upstream, long_taps,
    )
    rows = groups + 3 * tiles * EDGE
    mixed_out, feat_grad, heads, sums = call(
        functools.partial(halo_kernel, members),
        [((chan, tok), BF), whole, ((3, EDGE, chan), BF), ((rows, TILE), F32)],
        [pltpu.VMEM((BLOCK, tok), F32), pltpu.VMEM((BLOCK, tok), F32)],
        marks, streams, w, feats, upstream, from_last, from_next, conv, back, long_taps, part, moves,
    )
    next_heads = step_back(heads, size)

    cube = lax.axis_size(CUBE)
    rest = lax.axis_size("zh")
    tp = lax.axis_size(TP)
    mine = jnp.sum(exchange(sums.reshape(cube, rows // cube, TILE), CUBE), axis=0)
    mine, feat_grad, next_heads = lax.optimization_barrier((mine, feat_grad, next_heads))
    mine = jnp.sum(exchange(jnp.broadcast_to(mine, (rest,) + mine.shape), "zh"), axis=0)
    (grad_streams,) = call(
        streams_kernel, [whole], [pltpu.VMEM(*shifts)], marks, w, feat_grad, next_heads
    )
    mine, grad_streams = lax.optimization_barrier((mine, grad_streams))
    total = exchange(jnp.broadcast_to(mine, (cube,) + mine.shape), CUBE).reshape(rows, TILE)
    (squares,) = call(squares_kernel, [((tp, EDGE, TILE), F32)], [], total)
    squares = exchange(squares, TP)
    entries = tp * (groups * taps + 3 * chan * short)
    grad_long, grad_short = call(
        functools.partial(scale_kernel, entries),
        [((groups, taps), F32), ((3, short, chan), F32)],
        [],
        total, squares,
    )
    return (mixed_out, grad_streams, grad_long, jnp.transpose(grad_short, (0, 2, 1)))


def solution(mesh):
    fine = Mesh(mesh.devices.reshape(4, 4, 4, 4, 2), ("x", "zh", "zl", "y", "c"))
    in_specs = (P(None, TP, SEQ), P(None, TP, None), P(TP, None), P(SEQ), P(TP, SEQ))
    out_specs = (P(TP, SEQ), P(None, TP, SEQ), P(TP, None), P(None, TP, None))
    return jax.shard_map(local, mesh=fine, in_specs=in_specs, out_specs=out_specs, check_vma=False)
```

time: 506 us -> 104 us (0.21)
  blocking collectives: 281 us -> 28.1 us
  local copies, waits for them, and re-layouts: 96.3 us -> 2.06 us
  other arithmetic: 58.7 us -> 0.03 us
  Pallas kernels: 0 us -> 28.8 us
  between operations: 16.6 us -> 0.76 us
  starting transfers between devices: 16.8 us -> 29.5 us
  matrix products: 9.96 us -> 0 us
  waiting for transfers between devices: 23.1 us -> 14 us
    psum x2 -> x0, blocking collectives: 281 us -> none  [the longest x1 230 us: local(): filt_total, short_total = lax.psum((filt_grad, short_grad), 'seq')]
    reshape x9 -> x0, local copies, waits for them, and re-layouts: 29.7 us -> none  [the longest x8 29.6 us: diagonal_sums(): folded = jnp.sum(flat.reshape(count, rows, width + 1), axis=1)]
    pallas_call x0 -> x6, Pallas kernels: none -> 28.8 us  [call(): pl.pallas_call(kernel, in_specs=[pl.BlockSpec(memory_space=pltpu.VMEM) fo...]
    all_to_all x0 -> x2, blocking collectives: none -> 28.1 us  [exchange(): return lax.all_to_all(pieces, axes, 0, 0)]
    convert_element_type x11 -> x0, other arithmetic: 23.8 us -> none  [the longest x1 8.83 us: local(): grad_streams = total.astype(jnp.bfloat16)]
    all_to_all x0 -> x2, starting transfers between devices: none -> 22.4 us  [exchange(): return lax.all_to_all(pieces, axes, 0, 0)]
    psum x1 -> x0, waiting for transfers between devices: 19.8 us -> none  [local(): filt_total, short_total = lax.psum((filt_grad, short_grad), 'seq')]
    another operation x24 -> x0, local copies, waits for them, and re-layouts: 16.3 us -> none  [the longest x16 16 us: band_table(): tiled = jnp.tile(base, (1, rows))[:, :rows * width]]
  transfers between devices with their start and end apart: 7 -> 5, of which waited for: 2 -> 3; matrix products, arithmetic and copies ran while one was open for 5% -> 0% of each run, Pallas kernels for 0% -> 8%
where the time goes in v2:
time: 104 us; the launch traced here: 103 us
  starting transfers between devices  29.5 us (28%)
  Pallas kernels  28.8 us (28%)
  blocking collectives  28.1 us (27%)
  waiting for transfers between devices  14 us (13%)
  local copies, waits for them, and re-layouts  2.06 us (2%)
    pallas_call x6, Pallas kernels, call(): pl.pallas_call(kernel, in_specs=[pl.BlockSpec(memory_space=pltpu.VMEM) fo...  28.8 us
    all_to_all x2, blocking collectives, exchange(): return lax.all_to_all(pieces, axes, 0, 0)  28.1 us
    all_to_all x2, starting transfers between devices, exchange(): return lax.all_to_all(pieces, axes, 0, 0)  22.4 us
    all_to_all x2, waiting for transfers between devices, exchange(): return lax.all_to_all(pieces, axes, 0, 0)  12.2 us
    ppermute x1, starting transfers between devices, step_forward(): return lax.ppermute(block, SEQ, [(i, i + 1) for i in range(size - 1)])  4.38 us
    ppermute x2, starting transfers between devices, step_back(): return lax.ppermute(block, SEQ, [(i + 1, i) for i in range(size - 1)])  2.76 us
  transfers between devices with their start and end apart: 5, of which 3 were waited for; matrix products, arithmetic and copies ran while one was open for 0% of the time, Pallas kernels for 8%

profile of v2, /device:TPU:1, one launch (start us, length us, event | category | flops | bytes accessed | tf_op | source)
XLA Modules:
  0.0 103.4 jit_solution(2987733094679772579)
XLA Ops:
  0.6 0.0 copy-start.1
  0.6 0.0 copy-start.3
  0.7 0.0 copy-start.4
  0.7 7.1 %shard_map.84 = (bf16[3,1024,256]{2,1,0:T(8,128)(2,1)}, bf16[1280,128]{1,0:T(8,128)(2,1)}, bf16[1152,128]{1,0:T(8,128)(2,1)}, bf16[1792,256]{1,0:T(8,128)(2,1)}) custom-call(s32[1,256]{1,0:T(1,128)} %bitcast.10, bf16[3,1024,256]{2,1,0:T(8,128)(2,1)} %x.3, f32[3,7,1024]{2,1,0:T(8,128)} %bitcast.7, bf16[1024,256]{1,0:T(8,128)(2,1)} %ups.5), custom_call_target="tpu_custom_call" | custom-call | flops 2000000000 | bytes 8000000 | tf_op jit(solution)/shard_map/pallas_call | solution.py:353
  7.7 4.4 %collective-permute-start = (bf16[1280,128]{1,0:T(8,128)(2,1)}, bf16[1280,128]{1,0:T(8,128)(2,1)S(1)}, u32[]{:S(2)}, u32[]{:S(2)}) collective-permute-start(bf16[1280,128]{1,0:T(8,128)(2,1)} %get-tuple-element.23), channel_id=1, source_target_pairs={{0,8},{8,16},{16,24},{24,32},{32,40},{40,48},{48,56},{56,64},{64,7... | collective-permute-start | bytes 983048 | tf_op jit(solution)/shard_map/ppermute | solution.py:367
  12.1 1.5 %collective-permute-start.1 = (bf16[1152,128]{1,0:T(8,128)(2,1)}, bf16[1152,128]{1,0:T(8,128)(2,1)S(1)}, u32[]{:S(2)}, u32[]{:S(2)}) collective-permute-start(bf16[1152,128]{1,0:T(8,128)(2,1)} %get-tuple-element.24), channel_id=1, source_target_pairs={{8,0},{16,8},{24,16},{32,24},{40,32},{48,40},{56,48},{64,56},{72,6... | collective-permute-start | bytes 884744 | tf_op jit(solution)/shard_map/ppermute | solution.py:371
  13.6 0.0 copy-done.1
  13.6 0.0 copy-done.3
  13.6 0.0 copy-done.4
  13.6 0.0 copy-start.5
  13.6 1.4 %copy-done.5 = bf16[3,1024,256]{2,1,0:T(8,128)(2,1)S(1)} copy-done((bf16[3,1024,256]{2,1,0:T(8,128)(2,1)S(1)}, bf16[3,1024,256]{2,1,0:T(8,128)(2,1)}, u32[]{:S(2)}) %copy-start.5) | copy-done | bytes 1572888
  15.0 0.0 copy-start
  15.0 0.0 copy-start.2
  15.0 0.0 copy-start.6
  15.0 3.1 %shard_map.85 = (f32[1024,128]{1,0:T(8,128)S(1)}, f32[1024,128]{1,0:T(8,128)S(1)}, f32[64,128]{1,0:T(8,128)S(1)}) custom-call(s32[1,256]{1,0:T(1,128)S(1)} %bitcast.11, bf16[3,1024,256]{2,1,0:T(8,128)(2,1)S(1)} %copy-done.5, bf16[1024,256]{1,0:T(8,128)(2,1)S(1)} %copy-done.1, f32[64,128]{1,0:T(8,128)S(1)} %copy-done.3), custom_call_target="tpu_custom_call" | custom-call | flops 2000000000 | bytes 8000000 | tf_op jit(solution)/shard_map/pallas_call | solution.py:353
  18.2 1.8 %collective-permute-done.1.from_next = bf16[1152,128]{1,0:T(8,128)(2,1)S(1)} collective-permute-done((bf16[1152,128]{1,0:T(8,128)(2,1)}, bf16[1152,128]{1,0:T(8,128)(2,1)S(1)}, u32[]{:S(2)}, u32[]{:S(2)}) %collective-permute-start.1) | collective-permute-done | bytes 294944 | tf_op jit(solution)/shard_map/ppermute | solution.py:371
  19.9 0.0 collective-permute-done.from_last
  19.9 0.0 copy-done
  19.9 0.0 copy-done.2
  20.0 0.0 copy-done.6
  20.0 12.5 %shard_map.86 = (bf16[1024,256]{1,0:T(8,128)(2,1)}, bf16[3,1024,256]{2,1,0:T(8,128)(2,1)S(1)}, bf16[3,8,1024]{2,1,0:T(8,128)(2,1)S(1)}, f32[256,128]{1,0:T(8,128)}) custom-call(s32[1,256]{1,0:T(1,128)S(1)} %bitcast.12, bf16[3,1024,256]{2,1,0:T(8,128)(2,1)S(1)} %copy-done, f32[3,7,1024]{2,1,0:T(8,128)S(1)} %bitcast.8, bf16[3,1024,256]{2,1,0:T(8,128)(2,1)S(1)} %copy-done.5, ...), custom_call_target="tpu_custom_call" | custom-call | flops 2000000000 | bytes 8000000 | tf_op jit(solution)/shard_map/pallas_call | solution.py:353
  32.4 12.4 %all-to-all-start = ((f32[16,16,128]{2,1,0:T(8,128)}), f32[16,16,128]{2,1,0:T(8,128)S(1)}, u32[]{:S(2)}, u32[]{:S(2)}) async-start(f32[16,16,128]{2,1,0:T(8,128)} %bitcast.2), calls=%async_computation | async-start | bytes 262144 | tf_op jit(solution)/shard_map/all_to_all | solution.py:375
  44.9 1.3 %collective-permute-start.2 = (bf16[3,8,1024]{2,1,0:T(8,128)(2,1)S(1)}, bf16[3,8,1024]{2,1,0:T(8,128)(2,1)S(1)}, u32[]{:S(2)}, u32[]{:S(2)}) collective-permute-start(bf16[3,8,1024]{2,1,0:T(8,128)(2,1)S(1)} %get-tuple-element.32), channel_id=1, source_target_pairs={{8,0},{16,8},{24,16},{32,24},{40,32},{48,40},{56,48},{64,56},{72,6... | collective-permute-start | bytes 147464 | tf_op jit(solution)/shard_map/ppermute | solution.py:371
  46.2 6.0 %all-to-all-done = f32[16,16,128]{2,1,0:T(8,128)S(1)} async-done(((f32[16,16,128]{2,1,0:T(8,128)}), f32[16,16,128]{2,1,0:T(8,128)S(1)}, u32[]{:S(2)}, u32[]{:S(2)}) %all-to-all-start) | async-done | bytes 131104 | tf_op jit(solution)/shard_map/all_to_all | solution.py:375
  52.2 0.0 collective-permute-done.2.next_heads
  52.2 0.6 broadcast_in_dim.6
  52.8 10.0 %all-to-all-start.1 = ((f32[4,16,128]{2,1,0:T(8,128)}), f32[4,16,128]{2,1,0:T(8,128)S(1)}, u32[]{:S(2)}, u32[]{:S(2)}) async-start(f32[4,16,128]{2,1,0:T(8,128)} %broadcast_in_dim.6), calls=%async_computation.1 | async-start | bytes 65536 | tf_op jit(solution)/shard_map/all_to_all | solution.py:375
  62.8 5.2 %shard_map.87 = bf16[3,1024,256]{2,1,0:T(8,128)(2,1)} custom-call(s32[1,256]{1,0:T(1,128)S(1)} %bitcast.13, f32[3,7,1024]{2,1,0:T(8,128)S(1)} %bitcast.9, bf16[3,1024,256]{2,1,0:T(8,128)(2,1)S(1)} %get-tuple-element.34.grads, bf16[3,8,1024]{2,1,0:T(8,128)(2,1)S(1)} %collective-permute-done.2.next_heads), custom_call_target="tpu_custom_call" | custom-call | flops 2000000000 | bytes 8000000 | tf_op jit(solution)/shard_map/pallas_call | solution.py:353
  68.0 6.3 %all-to-all-done.1 = f32[4,16,128]{2,1,0:T(8,128)S(1)} async-done(((f32[4,16,128]{2,1,0:T(8,128)}), f32[4,16,128]{2,1,0:T(8,128)S(1)}, u32[]{:S(2)}, u32[]{:S(2)}) %all-to-all-start.1) | async-done | bytes 32800 | tf_op jit(solution)/shard_map/all_to_all | solution.py:375
  74.3 12.7 %all_to_all.20 = f32[16,16,128]{2,1,0:T(8,128)S(1)} all-to-all(f32[16,16,128]{2,1,0:T(8,128)S(1)} %broadcast_in_dim.7), channel_id=1, replica_groups=mesh['x'=4,'zh'=4,'zl'=4,'y'=4,'c'=2] {'x','zl'}, dimensions={0} | all-to-all | bytes 262144 | tf_op jit(solution)/shard_map/all_to_all | solution.py:375
  87.1 0.2 shard_map.88
  87.2 15.4 %all_to_all.21.squares = f32[8,8,128]{2,1,0:T(8,128)S(1)} all-to-all(f32[8,8,128]{2,1,0:T(8,128)S(1)} %shard_map.88), channel_id=1, replica_groups=mesh['x'=4,'zh'=4,'zl'=4,'y'=4,'c'=2] {'y','c'}, dimensions={0} | all-to-all | bytes 65536 | tf_op jit(solution)/shard_map/all_to_all | solution.py:375
  102.6 0.8 shard_map.89
  (3 shorter events, 0.0 us)
Async XLA Ops:
  0.6 12.9 %copy-start.1 = (bf16[1024,256]{1,0:T(8,128)(2,1)S(1)}, bf16[1024,256]{1,0:T(8,128)(2,1)}, u32[]{:S(2)}) copy-start(bf16[1024,256]{1,0:T(8,128)(2,1)} %ups.5) | copy-start | bytes 1572868
  0.6 12.9 %copy-start.3 = (f32[64,128]{1,0:T(8,128)S(1)}, f32[64,128]{1,0:T(8,128)}, u32[]{:S(2)}) copy-start(f32[64,128]{1,0:T(8,128)} %filt.3) | copy-start | bytes 98308
  0.7 12.9 %copy-start.4 = (s32[256]{0:T(256)S(1)}, s32[256]{0:T(256)}, u32[]{:S(2)}) copy-start(s32[256]{0:T(256)} %param.8) | copy-start | bytes 3076
  7.7 12.2 %collective-permute-start = (bf16[1280,128]{1,0:T(8,128)(2,1)}, bf16[1280,128]{1,0:T(8,128)(2,1)S(1)}, u32[]{:S(2)}, u32[]{:S(2)}) collective-permute-start(bf16[1280,128]{1,0:T(8,128)(2,1)} %get-tuple-element.23), channel_id=1, source_target_pairs={{0,8},{8,16},{16,24},{24,32},{32,40},{40,48},{48,56},{56,64},{64,7... | collective-permute-start | bytes 983048 | tf_op jit(solution)/shard_map/ppermute | solution.py:367
  12.1 7.8 %collective-permute-start.1 = (bf16[1152,128]{1,0:T(8,128)(2,1)}, bf16[1152,128]{1,0:T(8,128)(2,1)S(1)}, u32[]{:S(2)}, u32[]{:S(2)}) collective-permute-start(bf16[1152,128]{1,0:T(8,128)(2,1)} %get-tuple-element.24), channel_id=1, source_target_pairs={{8,0},{16,8},{24,16},{32,24},{40,32},{48,40},{56,48},{64,56},{72,6... | collective-permute-start | bytes 884744 | tf_op jit(solution)/shard_map/ppermute | solution.py:371
  13.6 1.4 %copy-start.5 = (bf16[3,1024,256]{2,1,0:T(8,128)(2,1)S(1)}, bf16[3,1024,256]{2,1,0:T(8,128)(2,1)}, u32[]{:S(2)}) copy-start(bf16[3,1024,256]{2,1,0:T(8,128)(2,1)} %get-tuple-element.22.feats) | copy-start | bytes 4718596
  15.0 4.9 %copy-start = (bf16[3,1024,256]{2,1,0:T(8,128)(2,1)S(1)}, bf16[3,1024,256]{2,1,0:T(8,128)(2,1)}, u32[]{:S(2)}) copy-start(bf16[3,1024,256]{2,1,0:T(8,128)(2,1)} %x.3) | copy-start | bytes 4718596
  15.0 4.9 %copy-start.2 = (f32[3,1024,7]{1,2,0:T(8,128)S(1)}, f32[3,1024,7]{1,2,0:T(8,128)}, u32[]{:S(2)}) copy-start(f32[3,1024,7]{1,2,0:T(8,128)} %param.6) | copy-start | bytes 258052
  15.0 4.9 %copy-start.6 = (bf16[1792,256]{1,0:T(8,128)(2,1)S(1)}, bf16[1792,256]{1,0:T(8,128)(2,1)}, u32[]{:S(2)}) copy-start(bf16[1792,256]{1,0:T(8,128)(2,1)} %get-tuple-element.28.shifts) | copy-start | bytes 2752516
  32.4 19.7 %all-to-all-start = ((f32[16,16,128]{2,1,0:T(8,128)}), f32[16,16,128]{2,1,0:T(8,128)S(1)}, u32[]{:S(2)}, u32[]{:S(2)}) async-start(f32[16,16,128]{2,1,0:T(8,128)} %bitcast.2), calls=%async_computation | async-start | bytes 262144 | tf_op jit(solution)/shard_map/all_to_all | solution.py:375
  44.9 7.3 %collective-permute-start.2 = (bf16[3,8,1024]{2,1,0:T(8,128)(2,1)S(1)}, bf16[3,8,1024]{2,1,0:T(8,128)(2,1)S(1)}, u32[]{:S(2)}, u32[]{:S(2)}) collective-permute-start(bf16[3,8,1024]{2,1,0:T(8,128)(2,1)S(1)} %get-tuple-element.32), channel_id=1, source_target_pairs={{8,0},{16,8},{24,16},{32,24},{40,32},{48,40},{56,48},{64,56},{72,6... | collective-permute-start | bytes 147464 | tf_op jit(solution)/shard_map/ppermute | solution.py:371
  52.8 21.5 %all-to-all-start.1 = ((f32[4,16,128]{2,1,0:T(8,128)}), f32[4,16,128]{2,1,0:T(8,128)S(1)}, u32[]{:S(2)}, u32[]{:S(2)}) async-start(f32[4,16,128]{2,1,0:T(8,128)} %broadcast_in_dim.6), calls=%async_computation.1 | async-start | bytes 65536 | tf_op jit(solution)/shard_map/all_to_all | solution.py:375

commit v3 on v2

--- a/solution.py
+++ b/solution.py
@@ -13,12 +13,13 @@
 SEQ = ("x", "zh", "zl")
 TP = ("y", "c")
 CUBE = ("x", "zl")
+FAR = ("zh", "y", "c")
 TILE = 128
 EDGE = 8
 PACK = 16
 BLOCK = 256
 LIMIT = 24 * 1024 * 1024
-FIRST_LIMIT = 57 * 1024 * 1024
+FIRST_LIMIT = 53 * 1024 * 1024
 
 
 def nt(left, right):
@@ -108,7 +109,7 @@
     return nt(eye, wide.astype(BF))
 
 
-def feats_kernel(marks, x, w, ups, feats, next_pack, last_pack, shifts):
+def feats_kernel(marks, x, w, ups, feats, next_pack, last_pack, shifts, mixed_late, gate_late):
     short = w.shape[1]
     chan, tok = ups.shape
     seg_col, seg_row, row, col = segments(marks)
@@ -132,10 +133,12 @@
             tails.append(nt(take_tail, raw)[0:EDGE])
         tails.append(jnp.zeros_like(tails[0]))
         mixed = outs[1][:, tok - TILE :] * outs[2][:, tok - TILE :]
+        mixed_late[span, :] = mixed.astype(BF)
         next_pack[span, :] = jnp.where(open_end[:, tok - TILE :], mixed, 0.0).astype(BF)
         up = ups[span]
-        gate = up[:, 0:TILE].astype(F32) * outs[0][:, 0:TILE]
-        last_pack[span, :] = jnp.where(open_start[:, 0:TILE], gate, 0.0).astype(BF)
+        gate = up.astype(F32) * outs[0]
+        gate_late[span, :] = gate[:, tok - TILE :].astype(BF)
+        last_pack[span, :] = jnp.where(open_start[:, 0:TILE], gate[:, 0:TILE], 0.0).astype(BF)
         heads = nt(take_head, up).astype(BF)
         pairs = [
             jnp.concatenate([tails[p], tails[p + 1]], axis=0).astype(BF) for p in (0, 2)
@@ -155,6 +158,15 @@
     return pltpu.roll(wide, 0, 1, stride=1, stride_axis=0).astype(BF)
 
 
+def turned_filters(filt):
+    row, col = grid_of(TILE, TILE)
+    return nn(filt[...].astype(BF), ones_where((row + col == TILE) | (row + col == 0)))
+
+
+def spread(block, picks):
+    return jnp.concatenate([block * pick for pick in picks], axis=0)
+
+
 def diagonals(product):
     moved = pltpu.roll(product, 1, 1, stride=1, stride_axis=0)
     return jnp.sum(moved, axis=0, keepdims=True)
@@ -165,30 +177,33 @@
     return ones_where((col >= start) & (col < start + members))
 
 
-def own_kernel(members, marks, feats, ups, filt, conv, back, part):
-    chan, tok = ups.shape
+def own_kernel(members, marks, mixed_late, gate_late, filt, conv, back, part):
+    chan = mixed_late.shape[0]
+    tok = marks.shape[1]
     seg_col, seg_row, row, col = segments(marks)
     flip = reversal()
     s = slice(TILE, tok)
     keep_bf = ones_where((seg_col[s, s] == seg_row[s, s]) & (col[s, s] >= row[s, s]))
     keep = nn(flip, keep_bf)
+    keep_tbf = ones_where((seg_col[s, s] == seg_row[s, s]) & (col[s, s] <= row[s, s]))
+    back_filt = turned_filters(filt)
     picks = [members_mask(p, members) for p in range(0, TILE, members)]
     for lo in range(0, chan, BLOCK):
         span = slice(lo, lo + BLOCK)
-        mixed = (feats[1, span, s].astype(F32) * feats[2, span, s].astype(F32)).astype(BF)
-        gate = (ups[span, s].astype(F32) * feats[0, span, s].astype(F32)).astype(BF)
+        mixed = mixed_late[span]
+        gate = gate_late[span]
         mixed_t = nt(flip, mixed).astype(BF)
-        for g in range(BLOCK // members):
-            n = lo // members + g
-            table = circulant(filt, n) * keep_bf
-            rows = slice(g * members, (g + 1) * members)
-            at = slice(lo + g * members, lo + (g + 1) * members)
-            cb = (g * members) // TILE
+        for cb in range(BLOCK // TILE):
             chans = slice(cb * TILE, (cb + 1) * TILE)
-            conv[at, :] = nn(mixed[rows], table)
-            back[at, :] = nt(gate[rows], table)
-            product = nn(mixed_t[:, chans] * picks[g % len(picks)], gate[chans])
-            part[n : n + 1, :] = diagonals(product * keep)
+            products = nn(spread(mixed_t[:, chans], picks), gate[chans])
+            for k in range(len(picks)):
+                g = cb * len(picks) + k
+                n = lo // members + g
+                rows = slice(g * members, (g + 1) * members)
+                at = slice(lo + g * members, lo + (g + 1) * members)
+                conv[at, :] = nn(mixed[rows], circulant(filt, n) * keep_bf)
+                back[at, :] = nn(gate[rows], circulant(back_filt, n) * keep_tbf)
+                part[n : n + 1, :] = diagonals(products[k * TILE : (k + 1) * TILE] * keep)
 
 
 def halo_kernel(
@@ -217,6 +232,9 @@
     s = slice(0, TILE)
     keep_bf = ones_where((seg_col[s, s] == seg_row[s, s]) & (col[s, s] >= row[s, s]))
     keep = nn(flip, keep_bf)
+    keep_tbf = ones_where((seg_col[s, s] == seg_row[s, s]) & (col[s, s] <= row[s, s]))
+    upper_tbf = ones_where(col_t > row_t)
+    back_filt = turned_filters(filt)
     open_start = seg_col[0:EDGE, 0:BLOCK] == 0
     head_row, head_col = grid_of(EDGE, tok)
     take_head = ones_where((head_col == head_row) & (first == 0))
@@ -254,29 +272,48 @@
         mixed_t = nt(flip, mixed0).astype(BF)
         whole_t = nt(flip, mixed_b).astype(BF)
         base = lo // BLOCK * stride
-        for g in range(per):
-            n = lo // members + g
-            table = circulant(filt, n)
-            diag = table * keep_bf
-            table = table * upper_bf
-            rows = slice(g * members, (g + 1) * members)
-            at = slice(lo + g * members, lo + (g + 1) * members)
-            cb = (g * members) // TILE
+        for cb in range(BLOCK // TILE):
             chans = slice(cb * TILE, (cb + 1) * TILE)
-            pick = picks[g % len(picks)]
-            ahead = nn(jnp.concatenate([mixed_h[rows], mixed0[rows]], axis=0), table)
-            conv_s[rows, 0:TILE] = nn(mixed_b[rows], diag) + ahead[0:members] * from_start[0]
-            conv_s[rows, TILE:] = conv[at] + ahead[members:] * from_start[1]
-            behind = nt(jnp.concatenate([gate1[rows], gate_h[rows]], axis=0), table)
-            back_s[rows, 0:TILE] = nt(gate_b[rows], diag) + behind[0:members] * to_end[0]
-            back_s[rows, TILE:] = back[at] + behind[members:] * to_end[1]
-            product = nn(lead_t[:, chans] * pick, gate0[chans]) + nn(
-                mixed_t[:, chans] * pick, gate1[chans]
+            both = jnp.concatenate(
+                [spread(lead_t[:, chans], picks), spread(mixed_t[:, chans], picks)], axis=1
             )
-            inner = nn(whole_t[:, chans] * pick, gate_b[chans])
-            sums[base + g : base + g + 1, :] = part[n : n + 1, :] + diagonals(
-                product * upper + inner * keep
-            )
+            products = nn(both, jnp.concatenate([gate0[chans], gate1[chans]], axis=0))
+            inners = nn(spread(whole_t[:, chans], picks), gate_b[chans])
+            for k in range(len(picks)):
+                g = cb * len(picks) + k
+                n = lo // members + g
+                table = circulant(filt, n)
+                diag = table * keep_bf
+                table = table * upper_bf
+                turned = circulant(back_filt, n)
+                diag_b = turned * keep_tbf
+                turned = turned * upper_tbf
+                rows = slice(g * members, (g + 1) * members)
+                at = slice(lo + g * members, lo + (g + 1) * members)
+                ahead = nn(
+                    jnp.concatenate([mixed_h[rows], mixed0[rows], mixed_b[rows]], axis=0),
+                    jnp.concatenate([table, diag], axis=1),
+                )
+                conv_s[rows, 0:TILE] = (
+                    ahead[2 * members :, TILE:] + ahead[0:members, 0:TILE] * from_start[0]
+                )
+                conv_s[rows, TILE:] = (
+                    conv[at] + ahead[members : 2 * members, 0:TILE] * from_start[1]
+                )
+                behind = nn(
+                    jnp.concatenate([gate1[rows], gate_h[rows], gate_b[rows]], axis=0),
+                    jnp.concatenate([turned, diag_b], axis=1),
+                )
+                back_s[rows, 0:TILE] = (
+                    behind[2 * members :, TILE:] + behind[0:members, 0:TILE] * to_end[0]
+                )
+                back_s[rows, TILE:] = (
+                    back[at] + behind[members : 2 * members, 0:TILE] * to_end[1]
+                )
+                spots = slice(k * TILE, (k + 1) * TILE)
+                sums[base + g : base + g + 1, :] = part[n : n + 1, :] + diagonals(
+                    products[spots] * upper + inners[spots] * keep
+                )
         conv_v = conv_s[...]
         back_v = back_s[...]
         mixed_out[span, :] = (feat[0] * conv_v).astype(BF)
@@ -326,15 +363,27 @@
             out[j, span, TILE:] = (total[:, TILE:] + nt(eye, wide.astype(BF))).astype(BF)
 
 
-def squares_kernel(total, out):
-    value = total[...]
-    out[...] = jnp.broadcast_to(jnp.sum(value * value), out.shape)
-
-
-def scale_kernel(entries, total, squares, grad_long, grad_short):
-    mean = jnp.sum(squares[:, 0, 0:1]) / entries
+def merge_kernel(me, pieces, out):
+    far = out.shape[0]
+    tp = me.shape[0]
+    rows = pieces.shape[1]
+    rest = pieces.shape[0] // tp
+    total = pieces[0:tp].astype(F32)
+    for z in range(1, rest):
+        total = total + pieces[z * tp : (z + 1) * tp].astype(F32)
+    own = jnp.sum(total * me[...], axis=0)
+    square = jnp.broadcast_to(jnp.sum(total * total), (out.shape[1] - rows, TILE))
+    for i in range(far):
+        out[i, 0:rows] = own
+        out[i, rows:] = square
+
+
+def scale_kernel(entries, shares, grad_long, grad_short):
+    rows = shares.shape[1] - EDGE
+    mean = jnp.sum(shares[:, rows, 0:1]) / entries
     wide = jnp.broadcast_to(mean, (EDGE, TILE))
     scale = jnp.minimum(1.0, 1.0 / jnp.sqrt(wide + 1e-06))[0:1]
+    total = jnp.concatenate([shares[i, 0:rows] for i in range(shares.shape[0])], axis=0)
     short = grad_short.shape[1]
     members = grad_short.shape[2] // grad_long.shape[0]
     per = BLOCK // members
@@ -387,11 +436,12 @@
     whole = ((3, chan, tok), BF)
     tiles = chan // TILE
 
-    feats, next_pack, last_pack, moves = call(
+    late = ((chan, TILE), BF)
+    feats, next_pack, last_pack, moves, mixed_late, gate_late = call(
         feats_kernel,
         [
             whole, ((chan + 2 * tiles * PACK, TILE), BF), ((chan + tiles * PACK, TILE), BF),
-            shifts,
+            shifts, late, late,
         ],
         [],
         marks, streams, w, upstream,
@@ -405,7 +455,7 @@
         functools.partial(own_kernel, members),
         [half, half, ((groups, taps), F32)],
         [],
-        marks, feats, upstream, long_taps,
+        marks, mixed_late, gate_late, long_taps,
     )
     rows = groups + 3 * tiles * EDGE
     mixed_out, feat_grad, heads, sums = call(
@@ -417,24 +467,26 @@
     next_heads = step_back(heads, size)
 
     cube = lax.axis_size(CUBE)
-    rest = lax.axis_size("zh")
     tp = lax.axis_size(TP)
-    mine = jnp.sum(exchange(sums.reshape(cube, rows // cube, TILE), CUBE), axis=0)
+    far = tp * lax.axis_size("zh")
+    share = rows // cube
+    mine = jnp.sum(exchange(sums.reshape(cube, share, TILE), CUBE), axis=0).astype(BF)
     mine, feat_grad, next_heads = lax.optimization_barrier((mine, feat_grad, next_heads))
-    mine = jnp.sum(exchange(jnp.broadcast_to(mine, (rest,) + mine.shape), "zh"), axis=0)
+    pieces = exchange(jnp.broadcast_to(mine, (far,) + mine.shape), FAR)
     (grad_streams,) = call(
         streams_kernel, [whole], [pltpu.VMEM(*shifts)], marks, w, feat_grad, next_heads
     )
-    mine, grad_streams = lax.optimization_barrier((mine, grad_streams))
-    total = exchange(jnp.broadcast_to(mine, (cube,) + mine.shape), CUBE).reshape(rows, TILE)
-    (squares,) = call(squares_kernel, [((tp, EDGE, TILE), F32)], [], total)
-    squares = exchange(squares, TP)
+    pieces, grad_streams = lax.optimization_barrier((pieces, grad_streams))
+    me = jnp.where(jnp.arange(tp) == lax.axis_index(TP), 1.0, 0.0).astype(F32)
+    me = jnp.broadcast_to(me[:, None, None], (tp, 1, TILE))
+    (payload,) = call(merge_kernel, [((cube, share + EDGE, TILE), F32)], [], me, pieces)
+    shares = exchange(payload, CUBE)
     entries = tp * (groups * taps + 3 * chan * short)
     grad_long, grad_short = call(
         functools.partial(scale_kernel, entries),
         [((groups, taps), F32), ((3, short, chan), F32)],
         [],
-        total, squares,
+        shares,
     )
     return (mixed_out, grad_streams, grad_long, jnp.transpose(grad_short, (0, 2, 1)))
 

time: 104 us -> 101 us (0.971)
  blocking collectives: 28.1 us -> 14.7 us
  starting transfers between devices: 29.5 us -> 36.1 us
  waiting for transfers between devices: 14 us -> 20.5 us
  Pallas kernels: 28.8 us -> 26.2 us
    all_to_all x2 -> x1, blocking collectives: 28.1 us -> 14.7 us  [exchange(): return lax.all_to_all(pieces, axes, 0, 0)]
    all_to_all x2, starting transfers between devices: 22.4 us -> 29 us  [exchange(): return lax.all_to_all(pieces, axes, 0, 0)]
    all_to_all x2, waiting for transfers between devices: 12.2 us -> 17.2 us  [exchange(): return lax.all_to_all(pieces, axes, 0, 0)]
    pallas_call x6, Pallas kernels: 28.8 us -> 26.2 us  [call(): pl.pallas_call(kernel, in_specs=[pl.BlockSpec(memory_space=pltpu.VMEM) fo...]
    ppermute x2, waiting for transfers between devices: 1.79 us -> 3.34 us  [step_back(): return lax.ppermute(block, SEQ, [(i + 1, i) for i in range(size - 1)])]
where the time goes in v3:
time: 101 us
  starting transfers between devices  36.1 us (36%)
  Pallas kernels  26.2 us (26%)
  waiting for transfers between devices  20.5 us (20%)
  blocking collectives  14.7 us (15%)
  local copies, waits for them, and re-layouts  2.35 us (2%)
    all_to_all x2, starting transfers between devices, exchange(): return lax.all_to_all(pieces, axes, 0, 0)  29 us
    pallas_call x6, Pallas kernels, call(): pl.pallas_call(kernel, in_specs=[pl.BlockSpec(memory_space=pltpu.VMEM) fo...  26.2 us
    all_to_all x2, waiting for transfers between devices, exchange(): return lax.all_to_all(pieces, axes, 0, 0)  17.2 us
    all_to_all x1, blocking collectives, exchange(): return lax.all_to_all(pieces, axes, 0, 0)  14.7 us
    ppermute x1, starting transfers between devices, step_forward(): return lax.ppermute(block, SEQ, [(i, i + 1) for i in range(size - 1)])  4.38 us
    ppermute x2, waiting for transfers between devices, step_back(): return lax.ppermute(block, SEQ, [(i + 1, i) for i in range(size - 1)])  3.34 us
    ppermute x2, starting transfers between devices, step_back(): return lax.ppermute(block, SEQ, [(i + 1, i) for i in range(size - 1)])  2.76 us
  transfers between devices with their start and end apart: 5, of which 3 were waited for; matrix products, arithmetic and copies ran while one was open for 0% of the time, Pallas kernels for 8%

profile of v3, /device:TPU:1, one launch (start us, length us, event | category | flops | bytes accessed | tf_op | source)
XLA Modules:
  0.0 100.7 jit_solution(15626292287998075753)
XLA Ops:
  0.6 0.0 copy-start.2
  0.6 0.9 copy-done.2
  1.5 0.0 copy-start.5
  1.5 0.7 copy-done.5
  2.2 0.0 copy-start.4
  2.2 7.2 %shard_map.84 = (bf16[3,1024,256]{2,1,0:T(8,128)(2,1)}, bf16[1280,128]{1,0:T(8,128)(2,1)}, bf16[1152,128]{1,0:T(8,128)(2,1)S(1)}, bf16[1792,256]{1,0:T(8,128)(2,...) custom-call(s32[1,256]{1,0:T(1,128)S(1)} %bitcast.7, bf16[3,1024,256]{2,1,0:T(8,128)(2,1)} %x.3, ...), custom_call_target="tpu_custom_call" | custom-call | flops 2000000000 | bytes 8000000 | tf_op jit(solution)/shard_map/pallas_call | solution.py:402
  9.4 4.4 %collective-permute-start = (bf16[1280,128]{1,0:T(8,128)(2,1)}, bf16[1280,128]{1,0:T(8,128)(2,1)S(1)}, u32[]{:S(2)}, u32[]{:S(2)}) collective-permute-start(bf16[1280,128]{1,0:T(8,128)(2,1)} %get-tuple-element.25), channel_id=1, source_target_pairs={{0,8},{8,16},{16,24},{24,32},{32,40},{40,48},{48,56},{56,64},{64,7... | collective-permute-start | bytes 983048 | tf_op jit(solution)/shard_map/ppermute | solution.py:416
  13.8 1.5 %collective-permute-start.1 = (bf16[1152,128]{1,0:T(8,128)(2,1)S(1)}, bf16[1152,128]{1,0:T(8,128)(2,1)S(1)}, u32[]{:S(2)}, u32[]{:S(2)}) collective-permute-start(bf16[1152,128]{1,0:T(8,128)(2,1)S(1)} %get-tuple-element.26), channel_id=1, source_target_pairs={{8,0},{16,8},{24,16},{32,24},{40,32},{48,40},{56,48},{64,56},{72,6... | collective-permute-start | bytes 884744 | tf_op jit(solution)/shard_map/ppermute | solution.py:420
  15.2 0.0 copy-done.4
  15.3 0.0 copy-start
  15.3 0.0 copy-start.1
  15.3 0.0 copy-start.7
  15.3 0.0 copy-start.8
  15.3 2.8 %shard_map.85 = (f32[1024,128]{1,0:T(8,128)S(1)}, f32[1024,128]{1,0:T(8,128)S(1)}, f32[64,128]{1,0:T(8,128)S(1)}) custom-call(s32[1,256]{1,0:T(1,128)S(1)} %bitcast.8, bf16[1024,128]{1,0:T(8,128)(2,1)S(1)} %get-tuple-element.27.mixed_late, bf16[1024,128]{1,0:T(8,128)(2,1)S(1)} %get-tuple-element.28.gate_late, f32[64,128]{1,0:T(8,128)S(1)} %copy-done.4), custom_call_target="tpu_custom_call" | custom-call | flops 2000000000 | bytes 8000000 | tf_op jit(solution)/shard_map/pallas_call | solution.py:402
  18.1 3.3 %collective-permute-done.1.from_next = bf16[1152,128]{1,0:T(8,128)(2,1)S(1)} collective-permute-done((bf16[1152,128]{1,0:T(8,128)(2,1)S(1)}, bf16[1152,128]{1,0:T(8,128)(2,1)S(1)}, u32[]{:S(2)}, u32[]{:S(2)}) %collective-permute-start.1) | collective-permute-done | bytes 294944 | tf_op jit(solution)/shard_map/ppermute | solution.py:420
  21.4 0.0 collective-permute-done.from_last
  21.4 0.0 copy-done
  21.4 0.0 copy-done.1
  21.4 0.0 copy-done.7
  21.4 0.0 copy-done.8
  21.4 0.0 copy-start.3
  21.4 0.0 copy-start.6
  21.5 10.1 %shard_map.86 = (bf16[1024,256]{1,0:T(8,128)(2,1)}, bf16[3,1024,256]{2,1,0:T(8,128)(2,1)S(1)}, bf16[3,8,1024]{2,1,0:T(8,128)(2,1)S(1)}, f32[256,128]{1,0:T(8,128)}) custom-call(s32[1,256]{1,0:T(1,128)S(1)} %bitcast.9, bf16[3,1024,256]{2,1,0:T(8,128)(2,1)S(1)} %copy-done, f32[3,7,1024]{2,1,0:T(8,128)S(1)} %bitcast.5, bf16[3,1024,256]{2,1,0:T(8,128)(2,1)S(1)} %copy-done.7, ...), custom_call_target="tpu_custom_call" | custom-call | flops 2000000000 | bytes 8000000 | tf_op jit(solution)/shard_map/pallas_call | solution.py:402
  31.5 12.4 %all-to-all-start = ((f32[16,16,128]{2,1,0:T(8,128)}), f32[16,16,128]{2,1,0:T(8,128)S(1)}, u32[]{:S(2)}, u32[]{:S(2)}) async-start(f32[16,16,128]{2,1,0:T(8,128)} %bitcast.2), calls=%async_computation | async-start | bytes 262144 | tf_op jit(solution)/shard_map/all_to_all | solution.py:424
  44.0 1.3 %collective-permute-start.2 = (bf16[3,8,1024]{2,1,0:T(8,128)(2,1)S(1)}, bf16[3,8,1024]{2,1,0:T(8,128)(2,1)S(1)}, u32[]{:S(2)}, u32[]{:S(2)}) collective-permute-start(bf16[3,8,1024]{2,1,0:T(8,128)(2,1)S(1)} %get-tuple-element.36), channel_id=1, source_target_pairs={{8,0},{16,8},{24,16},{32,24},{40,32},{48,40},{56,48},{64,56},{72,6... | collective-permute-start | bytes 147464 | tf_op jit(solution)/shard_map/ppermute | solution.py:420
  45.3 6.0 %all-to-all-done = f32[16,16,128]{2,1,0:T(8,128)S(1)} async-done(((f32[16,16,128]{2,1,0:T(8,128)}), f32[16,16,128]{2,1,0:T(8,128)S(1)}, u32[]{:S(2)}, u32[]{:S(2)}) %all-to-all-start) | async-done | bytes 131104 | tf_op jit(solution)/shard_map/all_to_all | solution.py:424
  51.3 0.0 collective-permute-done.2.next_heads
  51.3 0.7 broadcast_in_dim.17
  51.9 16.6 %all-to-all-start.1 = ((bf16[32,16,128]{2,1,0:T(8,128)(2,1)}), bf16[32,16,128]{2,1,0:T(8,128)(2,1)S(1)}, u32[]{:S(2)}, u32[]{:S(2)}) async-start(bf16[32,16,128]{2,1,0:T(8,128)(2,1)} %broadcast_in_dim.17), calls=%async_computation.1 | async-start | bytes 262144 | tf_op jit(solution)/shard_map/all_to_all | solution.py:424
  68.5 0.0 copy-done.3
  68.5 0.0 copy-done.6
  68.5 5.2 %shard_map.87 = bf16[3,1024,256]{2,1,0:T(8,128)(2,1)} custom-call(s32[1,256]{1,0:T(1,128)S(1)} %bitcast.10, f32[3,7,1024]{2,1,0:T(8,128)S(1)} %bitcast.6, bf16[3,1024,256]{2,1,0:T(8,128)(2,1)S(1)} %get-tuple-element.38.grads, bf16[3,8,1024]{2,1,0:T(8,128)(2,1)S(1)} %collective-permute-done.2.next_heads), custom_call_target="tpu_custom_call" | custom-call | flops 2000000000 | bytes 8000000 | tf_op jit(solution)/shard_map/pallas_call | solution.py:402
  73.8 11.2 %all-to-all-done.1.pieces = bf16[32,16,128]{2,1,0:T(8,128)(2,1)S(1)} async-done(((bf16[32,16,128]{2,1,0:T(8,128)(2,1)}), bf16[32,16,128]{2,1,0:T(8,128)(2,1)S(1)}, u32[]{:S(2)}, u32[]{:S(2)}) %all-to-all-start.1) | async-done | bytes 131104 | tf_op jit(solution)/shard_map/all_to_all | solution.py:424
  85.0 0.1 broadcast_in_dim.20.me
  85.1 0.2 shard_map.88
  85.2 14.7 %all_to_all.15.shares = f32[16,24,128]{2,1,0:T(8,128)S(1)} all-to-all(f32[16,24,128]{2,1,0:T(8,128)S(1)} %shard_map.88), channel_id=1, replica_groups=mesh['x'=4,'zh'=4,'zl'=4,'y'=4,'c'=2] {'x','zl'}, dimensions={0} | all-to-all | bytes 393216 | tf_op jit(solution)/shard_map/all_to_all | solution.py:424
  99.9 0.8 shard_map.89
  (2 shorter events, 0.0 us)
Async XLA Ops:
  0.6 0.9 copy-start.2
  1.5 0.7 copy-start.5
  2.2 13.0 %copy-start.4 = (f32[64,128]{1,0:T(8,128)S(1)}, f32[64,128]{1,0:T(8,128)}, u32[]{:S(2)}) copy-start(f32[64,128]{1,0:T(8,128)} %filt.3) | copy-start | bytes 98308
  9.4 12.0 %collective-permute-start = (bf16[1280,128]{1,0:T(8,128)(2,1)}, bf16[1280,128]{1,0:T(8,128)(2,1)S(1)}, u32[]{:S(2)}, u32[]{:S(2)}) collective-permute-start(bf16[1280,128]{1,0:T(8,128)(2,1)} %get-tuple-element.25), channel_id=1, source_target_pairs={{0,8},{8,16},{16,24},{24,32},{32,40},{40,48},{48,56},{56,64},{64,7... | collective-permute-start | bytes 983048 | tf_op jit(solution)/shard_map/ppermute | solution.py:416
  13.8 7.6 %collective-permute-start.1 = (bf16[1152,128]{1,0:T(8,128)(2,1)S(1)}, bf16[1152,128]{1,0:T(8,128)(2,1)S(1)}, u32[]{:S(2)}, u32[]{:S(2)}) collective-permute-start(bf16[1152,128]{1,0:T(8,128)(2,1)S(1)} %get-tuple-element.26), channel_id=1, source_target_pairs={{8,0},{16,8},{24,16},{32,24},{40,32},{48,40},{56,48},{64,56},{72,6... | collective-permute-start | bytes 884744 | tf_op jit(solution)/shard_map/ppermute | solution.py:420
  15.3 6.2 %copy-start = (bf16[3,1024,256]{2,1,0:T(8,128)(2,1)S(1)}, bf16[3,1024,256]{2,1,0:T(8,128)(2,1)}, u32[]{:S(2)}) copy-start(bf16[3,1024,256]{2,1,0:T(8,128)(2,1)} %x.3) | copy-start | bytes 4718596
  15.3 6.1 %copy-start.1 = (bf16[1024,256]{1,0:T(8,128)(2,1)S(1)}, bf16[1024,256]{1,0:T(8,128)(2,1)}, u32[]{:S(2)}) copy-start(bf16[1024,256]{1,0:T(8,128)(2,1)} %ups.3) | copy-start | bytes 1572868
  15.3 6.1 %copy-start.7 = (bf16[3,1024,256]{2,1,0:T(8,128)(2,1)S(1)}, bf16[3,1024,256]{2,1,0:T(8,128)(2,1)}, u32[]{:S(2)}) copy-start(bf16[3,1024,256]{2,1,0:T(8,128)(2,1)} %get-tuple-element.24.feats) | copy-start | bytes 4718596
  15.3 6.1 %copy-start.8 = (bf16[1792,256]{1,0:T(8,128)(2,1)S(1)}, bf16[1792,256]{1,0:T(8,128)(2,1)}, u32[]{:S(2)}) copy-start(bf16[1792,256]{1,0:T(8,128)(2,1)} %get-tuple-element.32.shifts) | copy-start | bytes 2752516
  21.4 47.1 %copy-start.3 = (f32[3,1024,7]{1,2,0:T(8,128)S(1)}, f32[3,1024,7]{1,2,0:T(8,128)}, u32[]{:S(2)}) copy-start(f32[3,1024,7]{1,2,0:T(8,128)} %param.6) | copy-start | bytes 258052
  21.4 47.1 %copy-start.6 = (s32[256]{0:T(256)S(1)}, s32[256]{0:T(256)}, u32[]{:S(2)}) copy-start(s32[256]{0:T(256)} %param.8) | copy-start | bytes 3076
  31.5 19.7 %all-to-all-start = ((f32[16,16,128]{2,1,0:T(8,128)}), f32[16,16,128]{2,1,0:T(8,128)S(1)}, u32[]{:S(2)}, u32[]{:S(2)}) async-start(f32[16,16,128]{2,1,0:T(8,128)} %bitcast.2), calls=%async_computation | async-start | bytes 262144 | tf_op jit(solution)/shard_map/all_to_all | solution.py:424
  44.0 7.3 %collective-permute-start.2 = (bf16[3,8,1024]{2,1,0:T(8,128)(2,1)S(1)}, bf16[3,8,1024]{2,1,0:T(8,128)(2,1)S(1)}, u32[]{:S(2)}, u32[]{:S(2)}) collective-permute-start(bf16[3,8,1024]{2,1,0:T(8,128)(2,1)S(1)} %get-tuple-element.36), channel_id=1, source_target_pairs={{8,0},{16,8},{24,16},{32,24},{40,32},{48,40},{56,48},{64,56},{72,6... | collective-permute-start | bytes 147464 | tf_op jit(solution)/shard_map/ppermute | solution.py:420
  51.9 33.1 %all-to-all-start.1 = ((bf16[32,16,128]{2,1,0:T(8,128)(2,1)}), bf16[32,16,128]{2,1,0:T(8,128)(2,1)S(1)}, u32[]{:S(2)}, u32[]{:S(2)}) async-start(bf16[32,16,128]{2,1,0:T(8,128)(2,1)} %broadcast_in_dim.17), calls=%async_computation.1 | async-start | bytes 262144 | tf_op jit(solution)/shard_map/all_to_all | solution.py:424

commit v4 on v3

--- a/solution.py
+++ b/solution.py
@@ -19,7 +19,7 @@
 PACK = 16
 BLOCK = 256
 LIMIT = 24 * 1024 * 1024
-FIRST_LIMIT = 53 * 1024 * 1024
+FIRST_LIMIT = 57 * 1024 * 1024
 
 
 def nt(left, right):
@@ -109,7 +109,7 @@
     return nt(eye, wide.astype(BF))
 
 
-def feats_kernel(marks, x, w, ups, feats, next_pack, last_pack, shifts, mixed_late, gate_late):
+def feats_kernel(marks, x, w, ups, feats, next_pack, last_pack, mixed_late, gate_late, shifts):
     short = w.shape[1]
     chan, tok = ups.shape
     seg_col, seg_row, row, col = segments(marks)
@@ -207,12 +207,13 @@
 
 
 def halo_kernel(
-    members, marks, x, w, feats, ups, from_last, from_next, conv, back, filt, part, shifts,
-    mixed_out, grads, heads, sums, conv_s, back_s,
+    members, marks, x, w, feats, ups, from_last, from_next, conv, back, filt, part,
+    mixed_out, grads, heads, sums_out, shifts, conv_s, back_s, sums,
 ):
     short = w.shape[1]
     chan, tok = ups.shape
     seg_col, seg_row, row, col = segments(marks)
+    fill_shifts(shifts, seg_col == seg_row, col - row, short)
     eye = identity(BLOCK)
     flip = reversal()
     first = seg_row[0:1, :]
@@ -341,6 +342,7 @@
             for h in range(BLOCK // TILE):
                 at = base + per + (j * (BLOCK // TILE) + h) * EDGE
                 sums[at : at + EDGE, :] = stacked[:, h * TILE : (h + 1) * TILE]
+    sums_out[...] = sums[...].astype(BF)
 
 
 def streams_kernel(marks, w, grads, next_heads, out, shifts):
@@ -371,19 +373,23 @@
     total = pieces[0:tp].astype(F32)
     for z in range(1, rest):
         total = total + pieces[z * tp : (z + 1) * tp].astype(F32)
-    own = jnp.sum(total * me[...], axis=0)
-    square = jnp.broadcast_to(jnp.sum(total * total), (out.shape[1] - rows, TILE))
+    own = jnp.sum(total * me[...], axis=0).astype(BF)
+    square = jnp.broadcast_to(jnp.sum(total * total), (PACK, TILE))
+    high = square.astype(BF).astype(F32)
+    row, _ = grid_of(PACK, TILE)
+    square = jnp.where(row == 0, high, jnp.where(row == 1, square - high, 0.0)).astype(BF)
     for i in range(far):
         out[i, 0:rows] = own
         out[i, rows:] = square
 
 
 def scale_kernel(entries, shares, grad_long, grad_short):
-    rows = shares.shape[1] - EDGE
-    mean = jnp.sum(shares[:, rows, 0:1]) / entries
+    rows = shares.shape[1] - PACK
+    extra = shares[:, rows:].astype(F32)
+    mean = jnp.sum(extra[:, :, 0:1]) / entries
     wide = jnp.broadcast_to(mean, (EDGE, TILE))
     scale = jnp.minimum(1.0, 1.0 / jnp.sqrt(wide + 1e-06))[0:1]
-    total = jnp.concatenate([shares[i, 0:rows] for i in range(shares.shape[0])], axis=0)
+    total = jnp.concatenate([shares[i, 0:rows].astype(F32) for i in range(shares.shape[0])], axis=0)
     short = grad_short.shape[1]
     members = grad_short.shape[2] // grad_long.shape[0]
     per = BLOCK // members
@@ -437,13 +443,13 @@
     tiles = chan // TILE
 
     late = ((chan, TILE), BF)
-    feats, next_pack, last_pack, moves, mixed_late, gate_late = call(
+    feats, next_pack, last_pack, mixed_late, gate_late = call(
         feats_kernel,
         [
             whole, ((chan + 2 * tiles * PACK, TILE), BF), ((chan + tiles * PACK, TILE), BF),
-            shifts, late, late,
+            late, late,
         ],
-        [],
+        [pltpu.VMEM(*shifts)],
         marks, streams, w, upstream,
         limit=FIRST_LIMIT,
     )
@@ -460,9 +466,12 @@
     rows = groups + 3 * tiles * EDGE
     mixed_out, feat_grad, heads, sums = call(
         functools.partial(halo_kernel, members),
-        [((chan, tok), BF), whole, ((3, EDGE, chan), BF), ((rows, TILE), F32)],
-        [pltpu.VMEM((BLOCK, tok), F32), pltpu.VMEM((BLOCK, tok), F32)],
-        marks, streams, w, feats, upstream, from_last, from_next, conv, back, long_taps, part, moves,
+        [((chan, tok), BF), whole, ((3, EDGE, chan), BF), ((rows, TILE), BF)],
+        [
+            pltpu.VMEM(*shifts), pltpu.VMEM((BLOCK, tok), F32), pltpu.VMEM((BLOCK, tok), F32),
+            pltpu.VMEM((rows, TILE), F32),
+        ],
+        marks, streams, w, feats, upstream, from_last, from_next, conv, back, long_taps, part,
     )
     next_heads = step_back(heads, size)
 
@@ -470,7 +479,8 @@
     tp = lax.axis_size(TP)
     far = tp * lax.axis_size("zh")
     share = rows // cube
-    mine = jnp.sum(exchange(sums.reshape(cube, share, TILE), CUBE), axis=0).astype(BF)
+    mine = exchange(sums.reshape(cube, share, TILE), CUBE).astype(F32)
+    mine = jnp.sum(mine, axis=0).astype(BF)
     mine, feat_grad, next_heads = lax.optimization_barrier((mine, feat_grad, next_heads))
     pieces = exchange(jnp.broadcast_to(mine, (far,) + mine.shape), FAR)
     (grad_streams,) = call(
@@ -479,7 +489,7 @@
     pieces, grad_streams = lax.optimization_barrier((pieces, grad_streams))
     me = jnp.where(jnp.arange(tp) == lax.axis_index(TP), 1.0, 0.0).astype(F32)
     me = jnp.broadcast_to(me[:, None, None], (tp, 1, TILE))
-    (payload,) = call(merge_kernel, [((cube, share + EDGE, TILE), F32)], [], me, pieces)
+    (payload,) = call(merge_kernel, [((cube, share + PACK, TILE), BF)], [], me, pieces)
     shares = exchange(payload, CUBE)
     entries = tp * (groups * taps + 3 * chan * short)
     grad_long, grad_short = call(

time: 101 us -> 98 us (0.970)
  waiting for transfers between devices: 20.5 us -> 18.4 us
  blocking collectives: 14.7 us -> 13.6 us
    ppermute x2, waiting for transfers between devices: 3.34 us -> 1.67 us  [step_back(): return lax.ppermute(block, SEQ, [(i + 1, i) for i in range(size - 1)])]
    all_to_all x1, blocking collectives: 14.7 us -> 13.6 us  [exchange(): return lax.all_to_all(pieces, axes, 0, 0)]
where the time goes in v4:
time: 98 us; the launch traced here: 97.6 us
  starting transfers between devices  36.1 us (37%)
  Pallas kernels  26 us (27%)
  waiting for transfers between devices  18.4 us (19%)
  blocking collectives  13.6 us (14%)
  local copies, waits for them, and re-layouts  2.66 us (3%)
    all_to_all x2, starting transfers between devices, exchange(): return lax.all_to_all(pieces, axes, 0, 0)  28.8 us
    pallas_call x6, Pallas kernels, call(): pl.pallas_call(kernel, in_specs=[pl.BlockSpec(memory_space=pltpu.VMEM) fo...  26 us
    all_to_all x2, waiting for transfers between devices, exchange(): return lax.all_to_all(pieces, axes, 0, 0)  16.7 us
    all_to_all x1, blocking collectives, exchange(): return lax.all_to_all(pieces, axes, 0, 0)  13.6 us
    ppermute x1, starting transfers between devices, step_forward(): return lax.ppermute(block, SEQ, [(i, i + 1) for i in range(size - 1)])  4.38 us
    ppermute x2, starting transfers between devices, step_back(): return lax.ppermute(block, SEQ, [(i + 1, i) for i in range(size - 1)])  2.99 us
  transfers between devices with their start and end apart: 5, of which 3 were waited for; matrix products, arithmetic and copies ran while one was open for 0% of the time, Pallas kernels for 8%

profile of v4, /device:TPU:1, one launch (start us, length us, event | category | flops | bytes accessed | tf_op | source)
XLA Modules:
  0.0 97.6 jit_solution(10843173172880261879)
XLA Ops:
  0.6 0.0 copy-start.3
  0.6 0.0 copy-start.4
  0.7 7.2 %shard_map.84 = (bf16[3,1024,256]{2,1,0:T(8,128)(2,1)}, bf16[1280,128]{1,0:T(8,128)(2,1)}, bf16[1152,128]{1,0:T(8,128)(2,1)}, bf16[1024,128]{1,0:T(8,128)(2,1)}, bf16[1024,128]{1,0:T(8,128)(2,1)}) custom-call(s32[1,256]{1,0:T(1,128)} %bitcast.7, bf16[3,1024,256]{2,1,0:T(8,128)(2,1)} %x.3, f32[3,7,1024]{2,1,0:T(8,128)} %bitcast.4, bf16[1024,256]{1,0:T(8,128)(2,1)} %ups.3), custom_call_target="tpu_custom_call" | custom-call | flops 2000000000 | bytes 8000000 | tf_op jit(solution)/shard_map/pallas_call | solution.py:408
  7.8 4.4 %collective-permute-start = (bf16[1280,128]{1,0:T(8,128)(2,1)}, bf16[1280,128]{1,0:T(8,128)(2,1)S(1)}, u32[]{:S(2)}, u32[]{:S(2)}) collective-permute-start(bf16[1280,128]{1,0:T(8,128)(2,1)} %get-tuple-element.24), channel_id=1, source_target_pairs={{0,8},{8,16},{16,24},{24,32},{32,40},{40,48},{48,56},{56,64},{64,7... | collective-permute-start | bytes 983048 | tf_op jit(solution)/shard_map/ppermute | solution.py:422
  12.2 1.5 %collective-permute-start.1 = (bf16[1152,128]{1,0:T(8,128)(2,1)}, bf16[1152,128]{1,0:T(8,128)(2,1)S(1)}, u32[]{:S(2)}, u32[]{:S(2)}) collective-permute-start(bf16[1152,128]{1,0:T(8,128)(2,1)} %get-tuple-element.25), channel_id=1, source_target_pairs={{8,0},{16,8},{24,16},{32,24},{40,32},{48,40},{56,48},{64,56},{72,6... | collective-permute-start | bytes 884744 | tf_op jit(solution)/shard_map/ppermute | solution.py:426
  13.7 0.0 copy-done.3
  13.7 0.0 copy-done.4
  13.7 0.0 copy-start.6
  13.7 0.9 copy-done.6
  14.7 0.0 copy-start.7
  14.7 0.9 copy-done.7
  15.6 0.0 copy-start
  15.6 0.0 copy-start.1
  15.6 0.0 copy-start.2
  15.6 0.0 copy-start.5
  15.6 2.8 %shard_map.85 = (f32[1024,128]{1,0:T(8,128)S(1)}, f32[1024,128]{1,0:T(8,128)S(1)}, f32[64,128]{1,0:T(8,128)S(1)}) custom-call(s32[1,256]{1,0:T(1,128)S(1)} %bitcast.8, bf16[1024,128]{1,0:T(8,128)(2,1)S(1)} %copy-done.6, bf16[1024,128]{1,0:T(8,128)(2,1)S(1)} %copy-done.7, f32[64,128]{1,0:T(8,128)S(1)} %copy-done.3), custom_call_target="tpu_custom_call" | custom-call | flops 2000000000 | bytes 8000000 | tf_op jit(solution)/shard_map/pallas_call | solution.py:408
  18.4 1.7 %collective-permute-done.1.from_next = bf16[1152,128]{1,0:T(8,128)(2,1)S(1)} collective-permute-done((bf16[1152,128]{1,0:T(8,128)(2,1)}, bf16[1152,128]{1,0:T(8,128)(2,1)S(1)}, u32[]{:S(2)}, u32[]{:S(2)}) %collective-permute-start.1) | collective-permute-done | bytes 294944 | tf_op jit(solution)/shard_map/ppermute | solution.py:426
  20.1 0.0 collective-permute-done.from_last
  20.1 0.0 copy-done
  20.1 0.0 copy-done.1
  20.1 0.0 copy-done.2
  20.1 0.0 copy-done.5
  20.1 9.9 %shard_map.86 = (bf16[1024,256]{1,0:T(8,128)(2,1)}, bf16[3,1024,256]{2,1,0:T(8,128)(2,1)S(1)}, bf16[3,8,1024]{2,1,0:T(8,128)(2,1)S(1)}, bf16[256,128]{1,0:T(8,128)(2,1)}) custom-call(s32[1,256]{1,0:T(1,128)S(1)} %bitcast.9, bf16[3,1024,256]{2,1,0:T(8,128)(2,1)S(1)} %copy-done, f32[3,7,1024]{2,1,0:T(8,128)S(1)} %bitcast.5, ...), custom_call_target="tpu_custom_call" | custom-call | flops 2000000000 | bytes 8000000 | tf_op jit(solution)/shard_map/pallas_call | solution.py:408
  30.0 12.4 %all-to-all-start = ((bf16[16,16,128]{2,1,0:T(8,128)(2,1)}), bf16[16,16,128]{2,1,0:T(8,128)(2,1)S(1)}, u32[]{:S(2)}, u32[]{:S(2)}) async-start(bf16[16,16,128]{2,1,0:T(8,128)(2,1)} %bitcast.2), calls=%async_computation | async-start | bytes 131072 | tf_op jit(solution)/shard_map/all_to_all | solution.py:430
  42.4 1.5 %collective-permute-start.2 = (bf16[3,8,1024]{2,1,0:T(8,128)(2,1)S(1)}, bf16[3,8,1024]{2,1,0:T(8,128)(2,1)S(1)}, u32[]{:S(2)}, u32[]{:S(2)}) collective-permute-start(bf16[3,8,1024]{2,1,0:T(8,128)(2,1)S(1)} %get-tuple-element.34), channel_id=1, source_target_pairs={{8,0},{16,8},{24,16},{32,24},{40,32},{48,40},{56,48},{64,56},{72,6... | collective-permute-start | bytes 147464 | tf_op jit(solution)/shard_map/ppermute | solution.py:426
  43.9 5.5 %all-to-all-done = bf16[16,16,128]{2,1,0:T(8,128)(2,1)S(1)} async-done(((bf16[16,16,128]{2,1,0:T(8,128)(2,1)}), bf16[16,16,128]{2,1,0:T(8,128)(2,1)S(1)}, u32[]{:S(2)}, u32[]{:S(2)}) %all-to-all-start) | async-done | bytes 65568 | tf_op jit(solution)/shard_map/all_to_all | solution.py:430
  49.4 0.0 collective-permute-done.2.next_heads
  49.4 0.7 broadcast_in_dim.17
  50.1 16.4 %all-to-all-start.1 = ((bf16[32,16,128]{2,1,0:T(8,128)(2,1)}), bf16[32,16,128]{2,1,0:T(8,128)(2,1)S(1)}, u32[]{:S(2)}, u32[]{:S(2)}) async-start(bf16[32,16,128]{2,1,0:T(8,128)(2,1)} %broadcast_in_dim.17), calls=%async_computation.1 | async-start | bytes 262144 | tf_op jit(solution)/shard_map/all_to_all | solution.py:430
  66.5 5.2 %shard_map.87 = bf16[3,1024,256]{2,1,0:T(8,128)(2,1)} custom-call(s32[1,256]{1,0:T(1,128)S(1)} %bitcast.10, f32[3,7,1024]{2,1,0:T(8,128)S(1)} %bitcast.6, bf16[3,1024,256]{2,1,0:T(8,128)(2,1)S(1)} %get-tuple-element.36.grads, bf16[3,8,1024]{2,1,0:T(8,128)(2,1)S(1)} %collective-permute-done.2.next_heads), custom_call_target="tpu_custom_call" | custom-call | flops 2000000000 | bytes 8000000 | tf_op jit(solution)/shard_map/pallas_call | solution.py:408
  71.7 11.3 %all-to-all-done.1.pieces = bf16[32,16,128]{2,1,0:T(8,128)(2,1)S(1)} async-done(((bf16[32,16,128]{2,1,0:T(8,128)(2,1)}), bf16[32,16,128]{2,1,0:T(8,128)(2,1)S(1)}, u32[]{:S(2)}, u32[]{:S(2)}) %all-to-all-start.1) | async-done | bytes 131104 | tf_op jit(solution)/shard_map/all_to_all | solution.py:430
  83.0 0.1 broadcast_in_dim.20.me
  83.0 0.2 shard_map.88
  83.2 13.6 %all_to_all.15.shares = bf16[16,32,128]{2,1,0:T(8,128)(2,1)S(1)} all-to-all(bf16[16,32,128]{2,1,0:T(8,128)(2,1)S(1)} %shard_map.88), channel_id=1, replica_groups=mesh['x'=4,'zh'=4,'zl'=4,'y'=4,'c'=2] {'x','zl'}, dimensions={0} | all-to-all | bytes 262144 | tf_op jit(solution)/shard_map/all_to_all | solution.py:430
  96.8 0.8 shard_map.89
  (2 shorter events, 0.0 us)
Async XLA Ops:
  0.6 13.1 %copy-start.3 = (f32[64,128]{1,0:T(8,128)S(1)}, f32[64,128]{1,0:T(8,128)}, u32[]{:S(2)}) copy-start(f32[64,128]{1,0:T(8,128)} %filt.3) | copy-start | bytes 98308
  0.6 13.1 %copy-start.4 = (s32[256]{0:T(256)S(1)}, s32[256]{0:T(256)}, u32[]{:S(2)}) copy-start(s32[256]{0:T(256)} %param.8) | copy-start | bytes 3076
  7.8 12.2 %collective-permute-start = (bf16[1280,128]{1,0:T(8,128)(2,1)}, bf16[1280,128]{1,0:T(8,128)(2,1)S(1)}, u32[]{:S(2)}, u32[]{:S(2)}) collective-permute-start(bf16[1280,128]{1,0:T(8,128)(2,1)} %get-tuple-element.24), channel_id=1, source_target_pairs={{0,8},{8,16},{16,24},{24,32},{32,40},{40,48},{48,56},{56,64},{64,7... | collective-permute-start | bytes 983048 | tf_op jit(solution)/shard_map/ppermute | solution.py:422
  12.2 7.8 %collective-permute-start.1 = (bf16[1152,128]{1,0:T(8,128)(2,1)}, bf16[1152,128]{1,0:T(8,128)(2,1)S(1)}, u32[]{:S(2)}, u32[]{:S(2)}) collective-permute-start(bf16[1152,128]{1,0:T(8,128)(2,1)} %get-tuple-element.25), channel_id=1, source_target_pairs={{8,0},{16,8},{24,16},{32,24},{40,32},{48,40},{56,48},{64,56},{72,6... | collective-permute-start | bytes 884744 | tf_op jit(solution)/shard_map/ppermute | solution.py:426
  13.7 1.0 copy-start.6
  14.7 0.9 copy-start.7
  15.6 4.4 %copy-start = (bf16[3,1024,256]{2,1,0:T(8,128)(2,1)S(1)}, bf16[3,1024,256]{2,1,0:T(8,128)(2,1)}, u32[]{:S(2)}) copy-start(bf16[3,1024,256]{2,1,0:T(8,128)(2,1)} %x.3) | copy-start | bytes 4718596
  15.6 4.4 %copy-start.1 = (bf16[1024,256]{1,0:T(8,128)(2,1)S(1)}, bf16[1024,256]{1,0:T(8,128)(2,1)}, u32[]{:S(2)}) copy-start(bf16[1024,256]{1,0:T(8,128)(2,1)} %ups.3) | copy-start | bytes 1572868
  15.6 4.5 %copy-start.2 = (f32[3,1024,7]{1,2,0:T(8,128)S(1)}, f32[3,1024,7]{1,2,0:T(8,128)}, u32[]{:S(2)}) copy-start(f32[3,1024,7]{1,2,0:T(8,128)} %param.6) | copy-start | bytes 258052
  15.6 4.5 %copy-start.5 = (bf16[3,1024,256]{2,1,0:T(8,128)(2,1)S(1)}, bf16[3,1024,256]{2,1,0:T(8,128)(2,1)}, u32[]{:S(2)}) copy-start(bf16[3,1024,256]{2,1,0:T(8,128)(2,1)} %get-tuple-element.23.feats) | copy-start | bytes 4718596
  30.0 19.4 %all-to-all-start = ((bf16[16,16,128]{2,1,0:T(8,128)(2,1)}), bf16[16,16,128]{2,1,0:T(8,128)(2,1)S(1)}, u32[]{:S(2)}, u32[]{:S(2)}) async-start(bf16[16,16,128]{2,1,0:T(8,128)(2,1)} %bitcast.2), calls=%async_computation | async-start | bytes 131072 | tf_op jit(solution)/shard_map/all_to_all | solution.py:430
  42.4 7.0 %collective-permute-start.2 = (bf16[3,8,1024]{2,1,0:T(8,128)(2,1)S(1)}, bf16[3,8,1024]{2,1,0:T(8,128)(2,1)S(1)}, u32[]{:S(2)}, u32[]{:S(2)}) collective-permute-start(bf16[3,8,1024]{2,1,0:T(8,128)(2,1)S(1)} %get-tuple-element.34), channel_id=1, source_target_pairs={{8,0},{16,8},{24,16},{32,24},{40,32},{48,40},{56,48},{64,56},{72,6... | collective-permute-start | bytes 147464 | tf_op jit(solution)/shard_map/ppermute | solution.py:426
  50.1 32.9 %all-to-all-start.1 = ((bf16[32,16,128]{2,1,0:T(8,128)(2,1)}), bf16[32,16,128]{2,1,0:T(8,128)(2,1)S(1)}, u32[]{:S(2)}, u32[]{:S(2)}) async-start(bf16[32,16,128]{2,1,0:T(8,128)(2,1)} %broadcast_in_dim.17), calls=%async_computation.1 | async-start | bytes 262144 | tf_op jit(solution)/shard_map/all_to_all | solution.py:430

commit v5 on v4

--- a/solution.py
+++ b/solution.py
@@ -481,7 +481,7 @@
     share = rows // cube
     mine = exchange(sums.reshape(cube, share, TILE), CUBE).astype(F32)
     mine = jnp.sum(mine, axis=0).astype(BF)
-    mine, feat_grad, next_heads = lax.optimization_barrier((mine, feat_grad, next_heads))
+    mine, feat_grad = lax.optimization_barrier((mine, feat_grad))
     pieces = exchange(jnp.broadcast_to(mine, (far,) + mine.shape), FAR)
     (grad_streams,) = call(
         streams_kernel, [whole], [pltpu.VMEM(*shifts)], marks, w, feat_grad, next_heads

time: 98 us -> 95.8 us (0.978)
  blocking collectives: 13.6 us -> 31.4 us
  starting transfers between devices: 36.1 us -> 23.7 us
  waiting for transfers between devices: 18.4 us -> 11 us
    all_to_all x1 -> x2, blocking collectives: 13.6 us -> 31.4 us  [exchange(): return lax.all_to_all(pieces, axes, 0, 0)]
    all_to_all x2 -> x1, starting transfers between devices: 28.8 us -> 16.6 us  [exchange(): return lax.all_to_all(pieces, axes, 0, 0)]
    all_to_all x2 -> x1, waiting for transfers between devices: 16.7 us -> 4.64 us  [exchange(): return lax.all_to_all(pieces, axes, 0, 0)]
    ppermute x2, waiting for transfers between devices: 1.67 us -> 6.38 us  [step_back(): return lax.ppermute(block, SEQ, [(i + 1, i) for i in range(size - 1)])]
  transfers between devices with their start and end apart: 5 -> 4, of which waited for: 3 -> 3; matrix products, arithmetic and copies ran while one was open for 0% -> 0% of each run, Pallas kernels for 8% -> 8%
where the time goes in v5:
time: 95.8 us; the launch traced here: 95.4 us
  blocking collectives  31.4 us (33%)
  Pallas kernels  25.8 us (27%)
  starting transfers between devices  23.7 us (25%)
  waiting for transfers between devices  11 us (11%)
  local copies, waits for them, and re-layouts  2.65 us (3%)
    all_to_all x2, blocking collectives, exchange(): return lax.all_to_all(pieces, axes, 0, 0)  31.4 us
    pallas_call x6, Pallas kernels, call(): pl.pallas_call(kernel, in_specs=[pl.BlockSpec(memory_space=pltpu.VMEM) fo...  25.8 us
    all_to_all x1, starting transfers between devices, exchange(): return lax.all_to_all(pieces, axes, 0, 0)  16.6 us
    ppermute x2, waiting for transfers between devices, step_back(): return lax.ppermute(block, SEQ, [(i + 1, i) for i in range(size - 1)])  6.38 us
    all_to_all x1, waiting for transfers between devices, exchange(): return lax.all_to_all(pieces, axes, 0, 0)  4.64 us
    ppermute x1, starting transfers between devices, step_forward(): return lax.ppermute(block, SEQ, [(i, i + 1) for i in range(size - 1)])  4.38 us
    ppermute x2, starting transfers between devices, step_back(): return lax.ppermute(block, SEQ, [(i + 1, i) for i in range(size - 1)])  2.76 us
  transfers between devices with their start and end apart: 4, of which 3 were waited for; matrix products, arithmetic and copies ran while one was open for 0% of the time, Pallas kernels for 8%

profile of v5, /device:TPU:1, one launch (start us, length us, event | category | flops | bytes accessed | tf_op | source)
XLA Modules:
  0.0 95.4 jit_solution(8791911632795719641)
XLA Ops:
  0.6 0.0 copy-start.3
  0.6 0.0 copy-start.4
  0.7 7.2 %shard_map.84 = (bf16[3,1024,256]{2,1,0:T(8,128)(2,1)}, bf16[1280,128]{1,0:T(8,128)(2,1)}, bf16[1152,128]{1,0:T(8,128)(2,1)}, bf16[1024,128]{1,0:T(8,128)(2,1)}, bf16[1024,128]{1,0:T(8,128)(2,1)}) custom-call(s32[1,256]{1,0:T(1,128)} %bitcast.8, bf16[3,1024,256]{2,1,0:T(8,128)(2,1)} %x.3, f32[3,7,1024]{2,1,0:T(8,128)} %bitcast.5, bf16[1024,256]{1,0:T(8,128)(2,1)} %ups.3), custom_call_target="tpu_custom_call" | custom-call | flops 2000000000 | bytes 8000000 | tf_op jit(solution)/shard_map/pallas_call | solution.py:408
  7.8 4.4 %collective-permute-start = (bf16[1280,128]{1,0:T(8,128)(2,1)}, bf16[1280,128]{1,0:T(8,128)(2,1)S(1)}, u32[]{:S(2)}, u32[]{:S(2)}) collective-permute-start(bf16[1280,128]{1,0:T(8,128)(2,1)} %get-tuple-element.23), channel_id=1, source_target_pairs={{0,8},{8,16},{16,24},{24,32},{32,40},{40,48},{48,56},{56,64},{64,7... | collective-permute-start | bytes 983048 | tf_op jit(solution)/shard_map/ppermute | solution.py:422
  12.2 1.5 %collective-permute-start.1 = (bf16[1152,128]{1,0:T(8,128)(2,1)}, bf16[1152,128]{1,0:T(8,128)(2,1)S(1)}, u32[]{:S(2)}, u32[]{:S(2)}) collective-permute-start(bf16[1152,128]{1,0:T(8,128)(2,1)} %get-tuple-element.24), channel_id=1, source_target_pairs={{8,0},{16,8},{24,16},{32,24},{40,32},{48,40},{56,48},{64,56},{72,6... | collective-permute-start | bytes 884744 | tf_op jit(solution)/shard_map/ppermute | solution.py:426
  13.7 0.0 copy-done.3
  13.7 0.0 copy-done.4
  13.7 0.0 copy-start.6
  13.7 0.9 copy-done.6
  14.7 0.0 copy-start.7
  14.7 0.9 copy-done.7
  15.6 0.0 copy-start
  15.6 0.0 copy-start.1
  15.6 0.0 copy-start.2
  15.6 0.0 copy-start.5
  15.6 2.8 %shard_map.85 = (f32[1024,128]{1,0:T(8,128)S(1)}, f32[1024,128]{1,0:T(8,128)S(1)}, f32[64,128]{1,0:T(8,128)S(1)}) custom-call(s32[1,256]{1,0:T(1,128)S(1)} %bitcast.9, bf16[1024,128]{1,0:T(8,128)(2,1)S(1)} %copy-done.6, bf16[1024,128]{1,0:T(8,128)(2,1)S(1)} %copy-done.7, f32[64,128]{1,0:T(8,128)S(1)} %copy-done.3), custom_call_target="tpu_custom_call" | custom-call | flops 2000000000 | bytes 8000000 | tf_op jit(solution)/shard_map/pallas_call | solution.py:408
  18.4 1.7 %collective-permute-done.1.from_next = bf16[1152,128]{1,0:T(8,128)(2,1)S(1)} collective-permute-done((bf16[1152,128]{1,0:T(8,128)(2,1)}, bf16[1152,128]{1,0:T(8,128)(2,1)S(1)}, u32[]{:S(2)}, u32[]{:S(2)}) %collective-permute-start.1) | collective-permute-done | bytes 294944 | tf_op jit(solution)/shard_map/ppermute | solution.py:426
  20.1 0.0 collective-permute-done.from_last
  20.1 0.0 copy-done
  20.1 0.0 copy-done.1
  20.1 0.0 copy-done.2
  20.1 0.0 copy-done.5
  20.1 9.6 %shard_map.86 = (bf16[1024,256]{1,0:T(8,128)(2,1)}, bf16[3,1024,256]{2,1,0:T(8,128)(2,1)S(1)}, bf16[3,8,1024]{2,1,0:T(8,128)(2,1)S(1)}, bf16[256,128]{1,0:T(8,128)(2,1)S(1)}) custom-call(s32[1,256]{1,0:T(1,128)S(1)} %bitcast.10, bf16[3,1024,256]{2,1,0:T(8,128)(2,1)S(1)} %copy-done, f32[3,7,1024]{2,1,0:T(8,128)S(1)} %bitcast.6, ...), custom_call_target="tpu_custom_call" | custom-call | flops 2000000000 | bytes 8000000 | tf_op jit(solution)/shard_map/pallas_call | solution.py:408
  29.7 19.2 %all_to_all.15 = bf16[16,16,128]{2,1,0:T(8,128)(2,1)S(1)} all-to-all(bf16[16,16,128]{2,1,0:T(8,128)(2,1)S(1)} %bitcast.4), channel_id=1, replica_groups=mesh['x'=4,'zh'=4,'zl'=4,'y'=4,'c'=2] {'x','zl'}, dimensions={0} | all-to-all | bytes 131072 | tf_op jit(solution)/shard_map/all_to_all | solution.py:430
  48.9 0.7 broadcast_in_dim.17
  49.6 16.6 %all-to-all-start.1 = ((bf16[32,16,128]{2,1,0:T(8,128)(2,1)}), bf16[32,16,128]{2,1,0:T(8,128)(2,1)S(1)}, u32[]{:S(2)}, u32[]{:S(2)}) async-start(bf16[32,16,128]{2,1,0:T(8,128)(2,1)} %broadcast_in_dim.17), calls=%async_computation.1 | async-start | bytes 262144 | tf_op jit(solution)/shard_map/all_to_all | solution.py:430
  66.2 1.3 %collective-permute-start.2 = (bf16[3,8,1024]{2,1,0:T(8,128)(2,1)S(1)}, bf16[3,8,1024]{2,1,0:T(8,128)(2,1)S(1)}, u32[]{:S(2)}, u32[]{:S(2)}) collective-permute-start(bf16[3,8,1024]{2,1,0:T(8,128)(2,1)S(1)} %get-tuple-element.35), channel_id=1, source_target_pairs={{8,0},{16,8},{24,16},{32,24},{40,32},{48,40},{56,48},{64,56},{72,6... | collective-permute-start | bytes 147464 | tf_op jit(solution)/shard_map/ppermute | solution.py:426
  67.5 4.7 %collective-permute-done.2.next_heads = bf16[3,8,1024]{2,1,0:T(8,128)(2,1)S(1)} collective-permute-done((bf16[3,8,1024]{2,1,0:T(8,128)(2,1)S(1)}, bf16[3,8,1024]{2,1,0:T(8,128)(2,1)S(1)}, u32[]{:S(2)}, u32[]{:S(2)}) %collective-permute-start.2) | collective-permute-done | bytes 49184 | tf_op jit(solution)/shard_map/ppermute | solution.py:426
  72.2 5.2 %shard_map.87 = bf16[3,1024,256]{2,1,0:T(8,128)(2,1)} custom-call(s32[1,256]{1,0:T(1,128)S(1)} %bitcast.11, f32[3,7,1024]{2,1,0:T(8,128)S(1)} %bitcast.7, bf16[3,1024,256]{2,1,0:T(8,128)(2,1)S(1)} %get-tuple-element.34.grads, bf16[3,8,1024]{2,1,0:T(8,128)(2,1)S(1)} %collective-permute-done.2.next_heads), custom_call_target="tpu_custom_call" | custom-call | flops 2000000000 | bytes 8000000 | tf_op jit(solution)/shard_map/pallas_call | solution.py:408
  77.4 4.6 %all-to-all-done.1.pieces = bf16[32,16,128]{2,1,0:T(8,128)(2,1)S(1)} async-done(((bf16[32,16,128]{2,1,0:T(8,128)(2,1)}), bf16[32,16,128]{2,1,0:T(8,128)(2,1)S(1)}, u32[]{:S(2)}, u32[]{:S(2)}) %all-to-all-start.1) | async-done | bytes 131104 | tf_op jit(solution)/shard_map/all_to_all | solution.py:430
  82.1 0.1 broadcast_in_dim.20.me
  82.2 0.2 shard_map.88
  82.3 12.2 %all_to_all.16.shares = bf16[16,32,128]{2,1,0:T(8,128)(2,1)S(1)} all-to-all(bf16[16,32,128]{2,1,0:T(8,128)(2,1)S(1)} %shard_map.88), channel_id=1, replica_groups=mesh['x'=4,'zh'=4,'zl'=4,'y'=4,'c'=2] {'x','zl'}, dimensions={0} | all-to-all | bytes 262144 | tf_op jit(solution)/shard_map/all_to_all | solution.py:430
  94.5 0.8 shard_map.89
  (2 shorter events, 0.0 us)
Async XLA Ops:
  0.6 13.1 %copy-start.3 = (f32[64,128]{1,0:T(8,128)S(1)}, f32[64,128]{1,0:T(8,128)}, u32[]{:S(2)}) copy-start(f32[64,128]{1,0:T(8,128)} %filt.3) | copy-start | bytes 98308
  0.6 13.1 %copy-start.4 = (s32[256]{0:T(256)S(1)}, s32[256]{0:T(256)}, u32[]{:S(2)}) copy-start(s32[256]{0:T(256)} %param.8) | copy-start | bytes 3076
  7.8 12.2 %collective-permute-start = (bf16[1280,128]{1,0:T(8,128)(2,1)}, bf16[1280,128]{1,0:T(8,128)(2,1)S(1)}, u32[]{:S(2)}, u32[]{:S(2)}) collective-permute-start(bf16[1280,128]{1,0:T(8,128)(2,1)} %get-tuple-element.23), channel_id=1, source_target_pairs={{0,8},{8,16},{16,24},{24,32},{32,40},{40,48},{48,56},{56,64},{64,7... | collective-permute-start | bytes 983048 | tf_op jit(solution)/shard_map/ppermute | solution.py:422
  12.2 7.8 %collective-permute-start.1 = (bf16[1152,128]{1,0:T(8,128)(2,1)}, bf16[1152,128]{1,0:T(8,128)(2,1)S(1)}, u32[]{:S(2)}, u32[]{:S(2)}) collective-permute-start(bf16[1152,128]{1,0:T(8,128)(2,1)} %get-tuple-element.24), channel_id=1, source_target_pairs={{8,0},{16,8},{24,16},{32,24},{40,32},{48,40},{56,48},{64,56},{72,6... | collective-permute-start | bytes 884744 | tf_op jit(solution)/shard_map/ppermute | solution.py:426
  13.7 1.0 copy-start.6
  14.7 0.9 copy-start.7
  15.6 4.4 %copy-start = (bf16[3,1024,256]{2,1,0:T(8,128)(2,1)S(1)}, bf16[3,1024,256]{2,1,0:T(8,128)(2,1)}, u32[]{:S(2)}) copy-start(bf16[3,1024,256]{2,1,0:T(8,128)(2,1)} %x.3) | copy-start | bytes 4718596
  15.6 4.4 %copy-start.1 = (bf16[1024,256]{1,0:T(8,128)(2,1)S(1)}, bf16[1024,256]{1,0:T(8,128)(2,1)}, u32[]{:S(2)}) copy-start(bf16[1024,256]{1,0:T(8,128)(2,1)} %ups.3) | copy-start | bytes 1572868
  15.6 4.5 %copy-start.2 = (f32[3,1024,7]{1,2,0:T(8,128)S(1)}, f32[3,1024,7]{1,2,0:T(8,128)}, u32[]{:S(2)}) copy-start(f32[3,1024,7]{1,2,0:T(8,128)} %param.6) | copy-start | bytes 258052
  15.6 4.5 %copy-start.5 = (bf16[3,1024,256]{2,1,0:T(8,128)(2,1)S(1)}, bf16[3,1024,256]{2,1,0:T(8,128)(2,1)}, u32[]{:S(2)}) copy-start(bf16[3,1024,256]{2,1,0:T(8,128)(2,1)} %get-tuple-element.22.feats) | copy-start | bytes 4718596
  49.6 32.5 %all-to-all-start.1 = ((bf16[32,16,128]{2,1,0:T(8,128)(2,1)}), bf16[32,16,128]{2,1,0:T(8,128)(2,1)S(1)}, u32[]{:S(2)}, u32[]{:S(2)}) async-start(bf16[32,16,128]{2,1,0:T(8,128)(2,1)} %broadcast_in_dim.17), calls=%async_computation.1 | async-start | bytes 262144 | tf_op jit(solution)/shard_map/all_to_all | solution.py:430
  66.2 6.0 %collective-permute-start.2 = (bf16[3,8,1024]{2,1,0:T(8,128)(2,1)S(1)}, bf16[3,8,1024]{2,1,0:T(8,128)(2,1)S(1)}, u32[]{:S(2)}, u32[]{:S(2)}) collective-permute-start(bf16[3,8,1024]{2,1,0:T(8,128)(2,1)S(1)} %get-tuple-element.35), channel_id=1, source_target_pairs={{8,0},{16,8},{24,16},{32,24},{40,32},{48,40},{56,48},{64,56},{72,6... | collective-permute-start | bytes 147464 | tf_op jit(solution)/shard_map/ppermute | solution.py:426

commit v6 on v5

--- a/solution.py
+++ b/solution.py
@@ -85,9 +85,11 @@
 
 def edge_rows(packed, first, j, lo):
     rows = []
-    for tile in range(lo // TILE, (lo + BLOCK) // TILE):
-        at = first + (2 * tile + j // 2) * PACK
-        rows.append(packed[at : at + PACK, :].astype(F32)[(j % 2) * EDGE : (j % 2 + 1) * EDGE])
+    for h in range(BLOCK // TILE):
+        slot = 3 * h + j
+        at = first + (lo // BLOCK * 3 + slot // 2) * PACK
+        half = slot % 2 * EDGE
+        rows.append(packed[at : at + PACK, :].astype(F32)[half : half + EDGE])
     return jnp.concatenate(rows, axis=1)
 
 
@@ -131,7 +133,6 @@
             feats[j, span] = out
             outs.append(out.astype(F32))
             tails.append(nt(take_tail, raw)[0:EDGE])
-        tails.append(jnp.zeros_like(tails[0]))
         mixed = outs[1][:, tok - TILE :] * outs[2][:, tok - TILE :]
         mixed_late[span, :] = mixed.astype(BF)
         next_pack[span, :] = jnp.where(open_end[:, tok - TILE :], mixed, 0.0).astype(BF)
@@ -139,17 +140,18 @@
         gate = up.astype(F32) * outs[0]
         gate_late[span, :] = gate[:, tok - TILE :].astype(BF)
         last_pack[span, :] = jnp.where(open_start[:, 0:TILE], gate[:, 0:TILE], 0.0).astype(BF)
-        heads = nt(take_head, up).astype(BF)
-        pairs = [
-            jnp.concatenate([tails[p], tails[p + 1]], axis=0).astype(BF) for p in (0, 2)
-        ]
-        for h in range(0, BLOCK, TILE):
-            tile = (lo + h) // TILE
-            at = chan + tile * PACK
-            last_pack[at : at + PACK, :] = heads[:, h : h + TILE]
-            for p in range(2):
-                at = chan + (2 * tile + p) * PACK
-                next_pack[at : at + PACK, :] = pairs[p][:, h : h + TILE]
+        heads = nt(take_head, up)[0:EDGE]
+        halves = [slice(h, h + TILE) for h in range(0, BLOCK, TILE)]
+        block = lo // BLOCK
+        at = chan + block * PACK
+        last_pack[at : at + PACK, :] = jnp.concatenate(
+            [heads[:, h] for h in halves], axis=0
+        ).astype(BF)
+        slots = [tails[j][:, h] for h in halves for j in range(3)]
+        for p in range(3):
+            at = chan + (block * 3 + p) * PACK
+            pair = jnp.concatenate(slots[2 * p : 2 * p + 2], axis=0)
+            next_pack[at : at + PACK, :] = pair.astype(BF)
 
 
 def circulant(filt, g):
@@ -261,13 +263,9 @@
         gate1 = (gate[:, TILE:] * from_start[1]).astype(BF)
         mixed_h = from_last[span]
         beyond = border_sum(w, 0, span, after(nt(take_tail, x[0, span])), True)
-        ups_head = jnp.concatenate(
-            [
-                from_next[at : at + PACK, :].astype(F32)[0:EDGE]
-                for at in range(chan + lo // TILE * PACK, chan + (lo + BLOCK) // TILE * PACK, PACK)
-            ],
-            axis=1,
-        )
+        at = chan + lo // BLOCK * PACK
+        packed = from_next[at : at + PACK, :].astype(F32)
+        ups_head = jnp.concatenate([packed[0:EDGE], packed[EDGE:]], axis=1)
         gate_h = (from_next[span].astype(F32) + at_front(ups_head * beyond, eye)).astype(BF)
         lead_t = nt(flip, mixed_h).astype(BF)
         mixed_t = nt(flip, mixed0).astype(BF)
@@ -441,12 +439,13 @@
     shifts = ((short * tok, tok), BF)
     whole = ((3, chan, tok), BF)
     tiles = chan // TILE
+    blocks = chan // BLOCK
 
     late = ((chan, TILE), BF)
     feats, next_pack, last_pack, mixed_late, gate_late = call(
         feats_kernel,
         [
-            whole, ((chan + 2 * tiles * PACK, TILE), BF), ((chan + tiles * PACK, TILE), BF),
+            whole, ((chan + 3 * blocks * PACK, TILE), BF), ((chan + blocks * PACK, TILE), BF),
             late, late,
         ],
         [pltpu.VMEM(*shifts)],

time: 95.8 us -> 95.4 us (level)
  no operation moved by 1% of the time
where the time goes in v6:
time: 95.4 us; the launch traced here: 95 us
  blocking collectives  31.2 us (33%)
  Pallas kernels  25.8 us (27%)
  starting transfers between devices  23.7 us (25%)
  waiting for transfers between devices  10.9 us (11%)
  local copies, waits for them, and re-layouts  2.65 us (3%)
    all_to_all x2, blocking collectives, exchange(): return lax.all_to_all(pieces, axes, 0, 0)  31.2 us
    pallas_call x6, Pallas kernels, call(): pl.pallas_call(kernel, in_specs=[pl.BlockSpec(memory_space=pltpu.VMEM) fo...  25.8 us
    all_to_all x1, starting transfers between devices, exchange(): return lax.all_to_all(pieces, axes, 0, 0)  16.6 us
    ppermute x2, waiting for transfers between devices, step_back(): return lax.ppermute(block, SEQ, [(i + 1, i) for i in range(size - 1)])  6.2 us
    all_to_all x1, waiting for transfers between devices, exchange(): return lax.all_to_all(pieces, axes, 0, 0)  4.65 us
    ppermute x1, starting transfers between devices, step_forward(): return lax.ppermute(block, SEQ, [(i, i + 1) for i in range(size - 1)])  4.38 us
    ppermute x2, starting transfers between devices, step_back(): return lax.ppermute(block, SEQ, [(i + 1, i) for i in range(size - 1)])  2.76 us
    unnamed x16, local copies, waits for them, and re-layouts  1.92 us
  transfers between devices with their start and end apart: 4, of which 3 were waited for; matrix products, arithmetic and copies ran while one was open for 0% of the time, Pallas kernels for 8%

profile of v6, /device:TPU:1, one launch (start us, length us, event | category | flops | bytes accessed | tf_op | source)
XLA Modules:
  0.0 95.0 jit_solution(13212466809509192821)
XLA Ops:
  0.6 0.0 copy-start.3
  0.6 0.0 copy-start.4
  0.7 7.2 %shard_map.84 = (bf16[3,1024,256]{2,1,0:T(8,128)(2,1)}, bf16[1216,128]{1,0:T(8,128)(2,1)}, bf16[1088,128]{1,0:T(8,128)(2,1)}, bf16[1024,128]{1,0:T(8,128)(2,1)}, bf16[1024,128]{1,0:T(8,128)(2,1)}) custom-call(s32[1,256]{1,0:T(1,128)} %bitcast.8, bf16[3,1024,256]{2,1,0:T(8,128)(2,1)} %x.3, f32[3,7,1024]{2,1,0:T(8,128)} %bitcast.5, bf16[1024,256]{1,0:T(8,128)(2,1)} %ups.3), custom_call_target="tpu_custom_call" | custom-call | flops 2000000000 | bytes 8000000 | tf_op jit(solution)/shard_map/pallas_call | solution.py:406
  7.8 4.4 %collective-permute-start = (bf16[1216,128]{1,0:T(8,128)(2,1)}, bf16[1216,128]{1,0:T(8,128)(2,1)S(1)}, u32[]{:S(2)}, u32[]{:S(2)}) collective-permute-start(bf16[1216,128]{1,0:T(8,128)(2,1)} %get-tuple-element.23), channel_id=1, source_target_pairs={{0,8},{8,16},{16,24},{24,32},{32,40},{40,48},{48,56},{56,64},{64,7... | collective-permute-start | bytes 933896 | tf_op jit(solution)/shard_map/ppermute | solution.py:420
  12.2 1.5 %collective-permute-start.1 = (bf16[1088,128]{1,0:T(8,128)(2,1)}, bf16[1088,128]{1,0:T(8,128)(2,1)S(1)}, u32[]{:S(2)}, u32[]{:S(2)}) collective-permute-start(bf16[1088,128]{1,0:T(8,128)(2,1)} %get-tuple-element.24), channel_id=1, source_target_pairs={{8,0},{16,8},{24,16},{32,24},{40,32},{48,40},{56,48},{64,56},{72,6... | collective-permute-start | bytes 835592 | tf_op jit(solution)/shard_map/ppermute | solution.py:424
  13.7 0.0 copy-done.3
  13.7 0.0 copy-done.4
  13.7 0.0 copy-start.6
  13.7 0.9 copy-done.6
  14.7 0.0 copy-start.7
  14.7 0.9 copy-done.7
  15.6 0.0 copy-start
  15.6 0.0 copy-start.1
  15.6 0.0 copy-start.2
  15.6 0.0 copy-start.5
  15.6 2.8 %shard_map.85 = (f32[1024,128]{1,0:T(8,128)S(1)}, f32[1024,128]{1,0:T(8,128)S(1)}, f32[64,128]{1,0:T(8,128)S(1)}) custom-call(s32[1,256]{1,0:T(1,128)S(1)} %bitcast.9, bf16[1024,128]{1,0:T(8,128)(2,1)S(1)} %copy-done.6, bf16[1024,128]{1,0:T(8,128)(2,1)S(1)} %copy-done.7, f32[64,128]{1,0:T(8,128)S(1)} %copy-done.3), custom_call_target="tpu_custom_call" | custom-call | flops 2000000000 | bytes 8000000 | tf_op jit(solution)/shard_map/pallas_call | solution.py:406
  18.4 1.5 %collective-permute-done.1.from_next = bf16[1088,128]{1,0:T(8,128)(2,1)S(1)} collective-permute-done((bf16[1088,128]{1,0:T(8,128)(2,1)}, bf16[1088,128]{1,0:T(8,128)(2,1)S(1)}, u32[]{:S(2)}, u32[]{:S(2)}) %collective-permute-start.1) | collective-permute-done | bytes 278560 | tf_op jit(solution)/shard_map/ppermute | solution.py:424
  19.9 0.0 collective-permute-done.from_last
  19.9 0.0 copy-done
  19.9 0.0 copy-done.1
  19.9 0.0 copy-done.2
  19.9 0.0 copy-done.5
  19.9 9.6 %shard_map.86 = (bf16[1024,256]{1,0:T(8,128)(2,1)}, bf16[3,1024,256]{2,1,0:T(8,128)(2,1)S(1)}, bf16[3,8,1024]{2,1,0:T(8,128)(2,1)S(1)}, bf16[256,128]{1,0:T(8,128)(2,1)S(1)}) custom-call(s32[1,256]{1,0:T(1,128)S(1)} %bitcast.10, bf16[3,1024,256]{2,1,0:T(8,128)(2,1)S(1)} %copy-done, f32[3,7,1024]{2,1,0:T(8,128)S(1)} %bitcast.6, ...), custom_call_target="tpu_custom_call" | custom-call | flops 2000000000 | bytes 8000000 | tf_op jit(solution)/shard_map/pallas_call | solution.py:406
  29.5 19.0 %all_to_all.15 = bf16[16,16,128]{2,1,0:T(8,128)(2,1)S(1)} all-to-all(bf16[16,16,128]{2,1,0:T(8,128)(2,1)S(1)} %bitcast.4), channel_id=1, replica_groups=mesh['x'=4,'zh'=4,'zl'=4,'y'=4,'c'=2] {'x','zl'}, dimensions={0} | all-to-all | bytes 131072 | tf_op jit(solution)/shard_map/all_to_all | solution.py:428
  48.6 0.7 broadcast_in_dim.17
  49.2 16.6 %all-to-all-start.1 = ((bf16[32,16,128]{2,1,0:T(8,128)(2,1)}), bf16[32,16,128]{2,1,0:T(8,128)(2,1)S(1)}, u32[]{:S(2)}, u32[]{:S(2)}) async-start(bf16[32,16,128]{2,1,0:T(8,128)(2,1)} %broadcast_in_dim.17), calls=%async_computation.1 | async-start | bytes 262144 | tf_op jit(solution)/shard_map/all_to_all | solution.py:428
  65.8 1.3 %collective-permute-start.2 = (bf16[3,8,1024]{2,1,0:T(8,128)(2,1)S(1)}, bf16[3,8,1024]{2,1,0:T(8,128)(2,1)S(1)}, u32[]{:S(2)}, u32[]{:S(2)}) collective-permute-start(bf16[3,8,1024]{2,1,0:T(8,128)(2,1)S(1)} %get-tuple-element.35), channel_id=1, source_target_pairs={{8,0},{16,8},{24,16},{32,24},{40,32},{48,40},{56,48},{64,56},{72,6... | collective-permute-start | bytes 147464 | tf_op jit(solution)/shard_map/ppermute | solution.py:424
  67.1 4.7 %collective-permute-done.2.next_heads = bf16[3,8,1024]{2,1,0:T(8,128)(2,1)S(1)} collective-permute-done((bf16[3,8,1024]{2,1,0:T(8,128)(2,1)S(1)}, bf16[3,8,1024]{2,1,0:T(8,128)(2,1)S(1)}, u32[]{:S(2)}, u32[]{:S(2)}) %collective-permute-start.2) | collective-permute-done | bytes 49184 | tf_op jit(solution)/shard_map/ppermute | solution.py:424
  71.8 5.2 %shard_map.87 = bf16[3,1024,256]{2,1,0:T(8,128)(2,1)} custom-call(s32[1,256]{1,0:T(1,128)S(1)} %bitcast.11, f32[3,7,1024]{2,1,0:T(8,128)S(1)} %bitcast.7, bf16[3,1024,256]{2,1,0:T(8,128)(2,1)S(1)} %get-tuple-element.34.grads, bf16[3,8,1024]{2,1,0:T(8,128)(2,1)S(1)} %collective-permute-done.2.next_heads), custom_call_target="tpu_custom_call" | custom-call | flops 2000000000 | bytes 8000000 | tf_op jit(solution)/shard_map/pallas_call | solution.py:406
  77.1 4.6 %all-to-all-done.1.pieces = bf16[32,16,128]{2,1,0:T(8,128)(2,1)S(1)} async-done(((bf16[32,16,128]{2,1,0:T(8,128)(2,1)}), bf16[32,16,128]{2,1,0:T(8,128)(2,1)S(1)}, u32[]{:S(2)}, u32[]{:S(2)}) %all-to-all-start.1) | async-done | bytes 131104 | tf_op jit(solution)/shard_map/all_to_all | solution.py:428
  81.7 0.1 broadcast_in_dim.20.me
  81.8 0.2 shard_map.88
  82.0 12.2 %all_to_all.16.shares = bf16[16,32,128]{2,1,0:T(8,128)(2,1)S(1)} all-to-all(bf16[16,32,128]{2,1,0:T(8,128)(2,1)S(1)} %shard_map.88), channel_id=1, replica_groups=mesh['x'=4,'zh'=4,'zl'=4,'y'=4,'c'=2] {'x','zl'}, dimensions={0} | all-to-all | bytes 262144 | tf_op jit(solution)/shard_map/all_to_all | solution.py:428
  94.2 0.8 shard_map.89
  (2 shorter events, 0.0 us)
Async XLA Ops:
  0.6 13.1 %copy-start.3 = (f32[64,128]{1,0:T(8,128)S(1)}, f32[64,128]{1,0:T(8,128)}, u32[]{:S(2)}) copy-start(f32[64,128]{1,0:T(8,128)} %filt.3) | copy-start | bytes 98308
  0.6 13.1 %copy-start.4 = (s32[256]{0:T(256)S(1)}, s32[256]{0:T(256)}, u32[]{:S(2)}) copy-start(s32[256]{0:T(256)} %param.8) | copy-start | bytes 3076
  7.8 12.1 %collective-permute-start = (bf16[1216,128]{1,0:T(8,128)(2,1)}, bf16[1216,128]{1,0:T(8,128)(2,1)S(1)}, u32[]{:S(2)}, u32[]{:S(2)}) collective-permute-start(bf16[1216,128]{1,0:T(8,128)(2,1)} %get-tuple-element.23), channel_id=1, source_target_pairs={{0,8},{8,16},{16,24},{24,32},{32,40},{40,48},{48,56},{56,64},{64,7... | collective-permute-start | bytes 933896 | tf_op jit(solution)/shard_map/ppermute | solution.py:420
  12.2 7.7 %collective-permute-start.1 = (bf16[1088,128]{1,0:T(8,128)(2,1)}, bf16[1088,128]{1,0:T(8,128)(2,1)S(1)}, u32[]{:S(2)}, u32[]{:S(2)}) collective-permute-start(bf16[1088,128]{1,0:T(8,128)(2,1)} %get-tuple-element.24), channel_id=1, source_target_pairs={{8,0},{16,8},{24,16},{32,24},{40,32},{48,40},{56,48},{64,56},{72,6... | collective-permute-start | bytes 835592 | tf_op jit(solution)/shard_map/ppermute | solution.py:424
  13.7 1.0 %copy-start.6 = (bf16[1024,128]{1,0:T(8,128)(2,1)S(1)}, bf16[1024,128]{1,0:T(8,128)(2,1)}, u32[]{:S(2)}) copy-start(bf16[1024,128]{1,0:T(8,128)(2,1)} %get-tuple-element.25.mixed_late) | copy-start | bytes 786436
  14.7 0.9 copy-start.7
  15.6 4.3 %copy-start = (bf16[3,1024,256]{2,1,0:T(8,128)(2,1)S(1)}, bf16[3,1024,256]{2,1,0:T(8,128)(2,1)}, u32[]{:S(2)}) copy-start(bf16[3,1024,256]{2,1,0:T(8,128)(2,1)} %x.3) | copy-start | bytes 4718596
  15.6 4.3 %copy-start.1 = (bf16[1024,256]{1,0:T(8,128)(2,1)S(1)}, bf16[1024,256]{1,0:T(8,128)(2,1)}, u32[]{:S(2)}) copy-start(bf16[1024,256]{1,0:T(8,128)(2,1)} %ups.3) | copy-start | bytes 1572868
  15.6 4.3 %copy-start.2 = (f32[3,1024,7]{1,2,0:T(8,128)S(1)}, f32[3,1024,7]{1,2,0:T(8,128)}, u32[]{:S(2)}) copy-start(f32[3,1024,7]{1,2,0:T(8,128)} %param.6) | copy-start | bytes 258052
  15.6 4.3 %copy-start.5 = (bf16[3,1024,256]{2,1,0:T(8,128)(2,1)S(1)}, bf16[3,1024,256]{2,1,0:T(8,128)(2,1)}, u32[]{:S(2)}) copy-start(bf16[3,1024,256]{2,1,0:T(8,128)(2,1)} %get-tuple-element.22.feats) | copy-start | bytes 4718596
  49.2 32.5 %all-to-all-start.1 = ((bf16[32,16,128]{2,1,0:T(8,128)(2,1)}), bf16[32,16,128]{2,1,0:T(8,128)(2,1)S(1)}, u32[]{:S(2)}, u32[]{:S(2)}) async-start(bf16[32,16,128]{2,1,0:T(8,128)(2,1)} %broadcast_in_dim.17), calls=%async_computation.1 | async-start | bytes 262144 | tf_op jit(solution)/shard_map/all_to_all | solution.py:428
  65.8 6.0 %collective-permute-start.2 = (bf16[3,8,1024]{2,1,0:T(8,128)(2,1)S(1)}, bf16[3,8,1024]{2,1,0:T(8,128)(2,1)S(1)}, u32[]{:S(2)}, u32[]{:S(2)}) collective-permute-start(bf16[3,8,1024]{2,1,0:T(8,128)(2,1)S(1)} %get-tuple-element.35), channel_id=1, source_target_pairs={{8,0},{16,8},{24,16},{32,24},{40,32},{48,40},{56,48},{64,56},{72,6... | collective-permute-start | bytes 147464 | tf_op jit(solution)/shard_map/ppermute | solution.py:424
